TPU v7x, 32 devices: a whole 2x2x4 slice. The times are simulated.
32 devices in a mesh: dp: 32 (over z, y, x, core), cent: 1.
Axes of the slice: x: 2, y: 2, z: 4, core: 2. Of those that a mesh axis runs over, the one named last changes fastest.
Arguments:
- hidden: bfloat16 [5632, 11008], P('dp', 'cent'), may hold values from -6 to 6
- residual: bfloat16 [5632, 4096], P('dp', 'cent'), may hold values from -6 to 6
- down_weight: bfloat16 [11008, 4096], P('cent', 'dp'), may hold values from -0.0546875 to 0.0546875
- gain: float32 [4096], P('cent'), may hold values from 0.1 to 1.9
- proj_weight: bfloat16 [4096, 1024], P('cent'), may hold values from -0.09375 to 0.09375
- centroids: bfloat16 [16384, 1024], P(('dp', 'cent')), may hold values from -24 to 24
Outputs:
- weighted: float32 [16384, 1024], P(('dp', 'cent'))
- counts: float32 [16384], P(('dp', 'cent'))
All inputs are finite; a program needn't handle non-finite values.
Results may differ from a plain program's by a relative error of at most 0.011.
Values may be sent and summed in bfloat16 or wider, within the bound.
No kernel may reach another device: no remote copies, remote signals or barrier semaphores. Data moves between devices by JAX's collectives and lax.ppermute only.
A program may use at most 192 MiB of HBM per device.

v0:
```python
import math

import jax
import jax.numpy as jnp
from jax import lax
from jax.sharding import PartitionSpec as P


def body(hidden, residual, down_weight, gain, proj_weight, centroids):
    partial_layer = jnp.dot(
        hidden,
        lax.all_gather(down_weight, "dp", axis=1, tiled=True),
        preferred_element_type=jnp.float32,
    )
    layer_out = lax.psum_scatter(partial_layer, "cent", scatter_dimension=1, tiled=True)
    normed = ((layer_out + residual.astype(jnp.float32)) * gain).astype(jnp.bfloat16)
    partial_embed = jnp.dot(normed, proj_weight, preferred_element_type=jnp.float32)
    embed_width = proj_weight.shape[1]
    embed_full = lax.psum(partial_embed, "cent")
    scaled = (
        embed_full * lax.rsqrt(jnp.mean(embed_full * embed_full, axis=1, keepdims=True) + 1e-06)
    ).astype(jnp.bfloat16)
    gathered = lax.all_gather(scaled, "dp", axis=0, tiled=True)
    inverse = 1.0 / (math.sqrt(embed_width) * 0.05)
    scores = (
        lax.dot_general(
            gathered, centroids, (((1,), (1,)), ((), ())), preferred_element_type=jnp.float32
        )
        * inverse
    )
    local_max = jnp.max(scores, axis=1)
    row_max = lax.pmax(local_max, ("dp", "cent"))
    row_total = lax.psum(jnp.sum(jnp.exp(scores - row_max[:, None]), axis=1), ("dp", "cent"))
    log_total = row_max + jnp.log(row_total)
    probability = jnp.exp(scores - log_total[:, None])
    scale_up = centroids.shape[0] * lax.axis_size("dp") * lax.axis_size("cent") / gathered.shape[0]
    counts = scale_up * jnp.sum(probability, axis=0)
    prob_low = probability.astype(jnp.bfloat16)
    weighted = scale_up * lax.dot_general(
        prob_low, gathered, (((0,), (0,)), ((), ())), preferred_element_type=jnp.float32
    )
    return (weighted, counts)


def solution(mesh):
    in_specs = (
        P("dp", "cent"),
        P("dp", "cent"),
        P("cent", "dp"),
        P("cent"),
        P("cent", None),
        P(("dp", "cent"), None),
    )
    out_specs = (P(("dp", "cent"), None), P(("dp", "cent")))
    return jax.shard_map(body, mesh=mesh, in_specs=in_specs, out_specs=out_specs, check_vma=False)
```

profile of v0, /device:TPU:0, one launch (start us, length us, event | category | flops | bytes accessed | tf_op | source)
XLA Modules:
  0.0 740.8 jit_solution(15155266663396443107)
XLA Ops:
  7.2 0.0 copy-start
  7.2 0.0 all-gather.3.cloned.1.call-start
  7.2 0.7 all-gather.3.cloned.1.call-update
  7.9 0.0 all-gather.5.cloned.1.call-start
  8.0 479.0 %all-gather.3.cloned.1.call-done = bf16[11008,4096]{1,0:T(8,128)(2,1)} async-done(((bf16[11008,128]{1,0:T(8,128)(2,1)}), bf16[11008,4096]{1,0:T(8,128)(2,1)}) %all-gather.3.cloned.1.call-update) | async-done | bytes 90177552 | tf_op jit(solution)/shard_map/all_gather | solution.py:12
  486.9 33.0 %fusion.6 = bf16[176,4096]{1,0:T(8,128)(2,1)S(1)} fusion(bf16[176,11008]{1,0:T(8,128)(2,1)} %param.6, bf16[11008,4096]{1,0:T(8,128)(2,1)} %all-gather.3.cloned.1.call-done, bf16[176,4096]{1,0:T(8,128)(2,1)} %param.7, f32[4096]{0:T(1024)} %param.9), kind=kOutput, calls=%fused_computation.9 | convolution fusion | flops 15874129920 | bytes 96952320 | tf_op jit(solution)/shard_map/dot_general | solution.py:10
  519.9 5.1 multiply_reduce_fusion
  525.1 0.9 multiply_convert_fusion
  526.0 0.0 all-gather.5.cloned.1.call-update
  526.0 89.1 %all-gather.5.cloned.1.call-done = bf16[5632,1024]{1,0:T(8,128)(2,1)} async-done(((bf16[176,1024]{1,0:T(8,128)(2,1)}), bf16[5632,1024]{1,0:T(8,128)(2,1)}) %all-gather.5.cloned.1.call-update) | async-done | bytes 11534352 | tf_op jit(solution)/shard_map/all_gather | solution.py:23
  615.1 0.0 copy-done
  615.1 13.2 %fusion.10 = (f32[5632]{0:T(1024)S(1)}, f32[5632,512]{0,1:T(8,128)}) fusion(bf16[5632,1024]{1,0:T(8,128)(2,1)} %all-gather.5.cloned.1.call-done, bf16[512,1024]{1,0:T(8,128)(2,1)S(1)} %copy-done), kind=kOutput, calls=%fused_computation.16 | convolution fusion | flops 5911341568 | bytes 24139776 | tf_op jit(solution)/shard_map/dot_general | solution.py:26
  628.3 39.0 %pmax.7 = f32[5632]{0:T(1024)S(1)} all-reduce(f32[5632]{0:T(1024)S(1)} %get-tuple-element.4), channel_id=1, replica_groups=mesh['dp'=32,'cent'=1] {'dp','cent'}, use_global_device_ids=true, to_apply=%region_2.0 | all-reduce | flops 5632 | bytes 45056 | tf_op jit(solution)/shard_map/pmax | solution.py:32
  667.3 6.0 exponential_reduce_fusion
  673.3 40.8 %psum.6 = f32[5632]{0:T(1024)S(1)} all-reduce(f32[5632]{0:T(1024)S(1)} %exponential_reduce_fusion), channel_id=1, replica_groups=mesh['dp'=32,'cent'=1] {'dp','cent'}, use_global_device_ids=true, to_apply=%region_4.0 | all-reduce | flops 5632 | bytes 45056 | tf_op jit(solution)/shard_map/psum | solution.py:33
  714.1 6.0 fusion
  720.1 0.6 broadcast_multiply_fusion
  720.7 13.3 %fusion.7 = f32[512,1024]{1,0:T(8,128)} fusion(bf16[5632,1024]{1,0:T(8,128)(2,1)} %all-gather.5.cloned.1.call-done, f32[5632,512]{0,1:T(8,128)} %get-tuple-element.5, f32[5632]{0:T(1024)S(1)} %log_add_fusion), kind=kOutput, calls=%fused_computation.10 | convolution fusion | flops 5911871488 | bytes 25188352 | tf_op jit(solution)/shard_map/dot_general | solution.py:39
  (2 shorter events, 0.0 us)
Async XLA Ops:
  7.2 607.9 %copy-start = (bf16[512,1024]{1,0:T(8,128)(2,1)S(1)}, bf16[512,1024]{1,0:T(8,128)(2,1)}, u32[]{:S(2)}) copy-start(bf16[512,1024]{1,0:T(8,128)(2,1)} %param.11) | copy-start | bytes 3145732
  7.2 479.7 %all-gather.3.cloned.1.call-start = ((), (), s32[]{:S(2)}) async-start(), calls=%async_computation | async-start | bytes 92995584 | tf_op jit(solution)/shard_map/all_gather | solution.py:12
  7.9 607.2 %all-gather.5.cloned.1.call-start = ((), (), s32[]{:S(2)}) async-start(), calls=%async_computation.1 | async-start | bytes 11894784 | tf_op jit(solution)/shard_map/all_gather | solution.py:23
Sparse Core Ops, SparseCore 0:
  9.5 477.3 all-gather.2
  526.1 88.9 all-gather.4
where the time goes:
time: 741 us
  waiting for transfers between devices  569 us (77%)
  blocking collectives  79.8 us (11%)
  matrix products  64.6 us (9%)
  between operations  14.1 us (2%)
  other arithmetic  13.5 us (2%)
    all_gather x1, waiting for transfers between devices, body(): lax.all_gather(down_weight, 'dp', axis=1, tiled=True)  479 us
    all_gather x1, waiting for transfers between devices, body(): gathered = lax.all_gather(scaled, 'dp', axis=0, tiled=True)  89.1 us
    psum x1, blocking collectives, body(): lax.psum(jnp.sum(jnp.exp(scores - row_max[:, None]), axis=1), ('dp', 'cen...  40.8 us
    pmax x1, blocking collectives, body(): row_max = lax.pmax(local_max, ('dp', 'cent'))  39 us
    dot_general x1, matrix products, body(): jnp.dot(hidden, lax.all_gather(down_weight, 'dp', axis=1, tiled=True), pr...  33 us
  transfers between devices with their start and end apart: 2, of which 2 were waited for; matrix products, arithmetic and copies ran while one was open for 0% of the time, Pallas kernels for 0%

commit v1 on v0

v1 whole, which is shorter than its diff:
```python
import math

import jax
import jax.numpy as jnp
from jax import lax
from jax.sharding import PartitionSpec as P


F32 = jnp.float32
BF16 = jnp.bfloat16


def dot(a, b):
    return jnp.dot(a, b, preferred_element_type=F32)


def make_body(n, plane, lines):
    line_bits = lines.bit_length() - 1

    def hop(v, k):
        return lax.ppermute(v, "dp", [(i, i ^ k) for i in range(n)])

    planes = [[z * plane + q for q in range(plane)] for z in range(lines)]

    def flips(v, bits):
        for a, bit in enumerate(bits):
            v = jnp.where(bit == 1, jnp.flip(v, a), v)
        return v

    def gather_plane(slot):
        half = slot.shape[0] // 2
        a, b = slot[:half], slot[half:]
        a = jnp.concatenate([a, hop(a, 2)])
        b = jnp.concatenate([b, hop(b, 4)])
        ay, bx = hop(a, 4), hop(b, 2)
        return jnp.concatenate([a, ay, b, bx])

    def plane_order(v, half):
        v = v.reshape(2, 2, 2, half)
        a, b = v[0], v[1]
        return jnp.concatenate([a, jnp.swapaxes(b, 0, 1)], axis=2)

    def plane_order_back(v, half):
        a, b = v[..., :half], v[..., half:]
        return jnp.stack([a, jnp.swapaxes(b, 0, 1)]).reshape(-1)

    def lse(parts):
        v = jnp.stack(parts)
        top = jnp.max(v, axis=0)
        return top + jnp.log(jnp.sum(jnp.exp(v - top), axis=0))

    def body(hidden, residual, down_weight, gain, proj_weight, centroids):
        me = lax.axis_index("dp")
        bits = [(me >> k) & 1 for k in range(n.bit_length() - 1)]
        z_bits = bits[::-1][:line_bits]
        rows, hid = hidden.shape
        share = hid // n
        feat = residual.shape[1]
        width = proj_weight.shape[1]

        z_dims = (2,) * line_bits
        blocks = hidden.reshape(rows, lines, plane, share).transpose(1, 2, 0, 3)
        blocks = flips(blocks.reshape(*z_dims, plane, rows, share), z_bits)
        blocks = blocks.reshape(lines, plane, rows, share).transpose(1, 0, 2, 3)
        blocks = lax.all_to_all(blocks, "dp", 0, 0, tiled=True, axis_index_groups=planes)

        down_rows = lax.all_to_all(down_weight, "dp", 0, 1, tiled=True)
        own = gain[:, None] * proj_weight.astype(F32)
        own_hi = own.astype(BF16)
        full = lax.all_gather(own, "cent", axis=0, tiled=True)
        full_hi = full.astype(BF16)
        full_lo = (full - full_hi.astype(F32)).astype(BF16)
        fold = (dot(down_rows, full_hi) + dot(down_rows, full_lo)).astype(BF16)
        direct = dot(residual, own_hi)

        pair = jnp.concatenate([centroids, hop(centroids, 1)])

        part = 0.0
        for k in range(lines):
            block = fold if k == 0 else hop(fold, k * plane)
            part = part + dot(blocks[:, k].reshape(plane * rows, share), block)
        part = part.astype(BF16).reshape(plane, rows, width)
        part = lax.all_to_all(part, "dp", 0, 0, tiled=True, axis_index_groups=planes)
        raw = jnp.sum(part.astype(F32), axis=0) + direct
        raw = lax.psum(raw, "cent")
        embed = (raw * lax.rsqrt(jnp.mean(raw * raw, axis=1, keepdims=True) + 1e-06)).astype(BF16)

        inverse = 1.0 / (math.sqrt(width) * 0.05)
        half = rows // 2
        slots = [gather_plane(embed if k == 0 else hop(embed, k * plane)) for k in range(lines)]
        scores, local = [], []
        for block in slots:
            s = lax.dot_general(block, pair, (((1,), (1,)), ((), ())), preferred_element_type=F32)
            s = s * inverse
            top = jnp.max(s, axis=1)
            scores.append(s)
            local.append(top + jnp.log(jnp.sum(jnp.exp(s - top[:, None]), axis=1)))

        v = jnp.stack([plane_order(x, half) for x in local])
        v = flips(v.reshape(*z_dims, 2, 2, rows), z_bits + [bits[2], bits[1]])
        v = lse([v] + [hop(v, k) for k in range(2, plane, 2)])
        v = lse([v] + [hop(v, k * plane) for k in range(1, lines)])
        if lax.axis_size("cent") > 1:
            top = lax.pmax(v, "cent")
            v = top + jnp.log(lax.psum(jnp.exp(v - top), "cent"))
        v = flips(v, z_bits + [bits[2], bits[1]]).reshape(lines, 2, 2, rows)

        counts, weighted = 0.0, 0.0
        for k in range(lines):
            total = plane_order_back(v[k], half)
            prob = jnp.exp(scores[k] - total[:, None])
            counts = counts + jnp.sum(prob, axis=0)
            weighted = weighted + lax.dot_general(
                prob.astype(BF16), slots[k], (((0,), (0,)), ((), ())), preferred_element_type=F32
            )
        cents = centroids.shape[0]
        scale_up = cents * n * lax.axis_size("cent") / (rows * n)
        far = hop(weighted[cents:].astype(BF16), 1)
        far_counts = hop(counts[cents:], 1)
        weighted = scale_up * (weighted[:cents] + far.astype(F32))
        counts = scale_up * (counts[:cents] + far_counts)
        return weighted, counts

    return body


def solution(mesh):
    n = mesh.shape["dp"]
    plane = 8
    lines = n // plane
    in_specs = (
        P("dp", "cent"),
        P("dp", "cent"),
        P("cent", "dp"),
        P("cent"),
        P("cent", None),
        P(("dp", "cent"), None),
    )
    out_specs = (P(("dp", "cent"), None), P(("dp", "cent")))
    return jax.shard_map(
        make_body(n, plane, lines), mesh=mesh, in_specs=in_specs, out_specs=out_specs, check_vma=False
    )
```

time: 741 us -> 375 us (0.51)
  waiting for transfers between devices: 569 us -> 179 us
  blocking collectives: 79.8 us -> 0 us
  starting transfers between devices: 0.08 us -> 61.9 us
  local copies, waits for them, and re-layouts: 0.01 us -> 46.5 us
  between operations: 14.1 us -> 1.5 us
  other arithmetic: 13.5 us -> 23 us
  matrix products: 64.6 us -> 56.8 us
    all_gather x2 -> x0, waiting for transfers between devices: 568 us -> none  [the longest x1 479 us: body(): lax.all_gather(down_weight, 'dp', axis=1, tiled=True)]
    all_to_all x0 -> x3, waiting for transfers between devices: none -> 109 us  [the longest x1 38.4 us: body(): down_rows = lax.all_to_all(down_weight, 'dp', 0, 1, tiled=True)]
    ppermute x0 -> x31, waiting for transfers between devices: none -> 70.8 us  [hop(): return lax.ppermute(v, 'dp', [(i, i ^ k) for i in range(n)])]
    ppermute x0 -> x31, starting transfers between devices: none -> 44.5 us  [hop(): return lax.ppermute(v, 'dp', [(i, i ^ k) for i in range(n)])]
    psum x1 -> x0, blocking collectives: 40.8 us -> none  [body(): lax.psum(jnp.sum(jnp.exp(scores - row_max[:, None]), axis=1), ('dp', 'cen...]
    pmax x1 -> x0, blocking collectives: 39 us -> none  [body(): row_max = lax.pmax(local_max, ('dp', 'cent'))]
    all_to_all x0 -> x3, starting transfers between devices: none -> 17.4 us  [the longest x1 7.42 us: body(): down_rows = lax.all_to_all(down_weight, 'dp', 0, 1, tiled=True)]
    unnamed x2 -> x56, local copies, waits for them, and re-layouts: 0.01 us -> 16.1 us
  transfers between devices with their start and end apart: 2 -> 34, of which waited for: 2 -> 14; matrix products, arithmetic and copies ran while one was open for 0% -> 24% of each run, Pallas kernels for 0% -> 0%
where the time goes in v1:
time: 375 us; the launch traced here: 369 us
  waiting for transfers between devices  179 us (48%)
  starting transfers between devices  61.9 us (17%)
  matrix products  56.8 us (15%)
  local copies, waits for them, and re-layouts  46.5 us (12%)
  other arithmetic  23 us (6%)
    ppermute x31, waiting for transfers between devices, hop(): return lax.ppermute(v, 'dp', [(i, i ^ k) for i in range(n)])  70.8 us
    ppermute x31, starting transfers between devices, hop(): return lax.ppermute(v, 'dp', [(i, i ^ k) for i in range(n)])  44.5 us
    all_to_all x1, waiting for transfers between devices, body(): down_rows = lax.all_to_all(down_weight, 'dp', 0, 1, tiled=True)  38.4 us
    all_to_all x1, waiting for transfers between devices, body(): lax.all_to_all(blocks, 'dp', 0, 0, tiled=True, axis_index_groups=planes)  35.5 us
    all_to_all x1, waiting for transfers between devices, body(): lax.all_to_all(part, 'dp', 0, 0, tiled=True, axis_index_groups=planes)  34.7 us
    dot_general x7, matrix products, dot(): return jnp.dot(a, b, preferred_element_type=F32)  29.3 us
    unnamed x56, local copies, waits for them, and re-layouts  16.1 us
    dot_general x4, matrix products, body(): lax.dot_general(prob.astype(BF16), slots[k], (((0,), (0,)), ((), ())), pr...  15.5 us
  transfers between devices with their start and end apart: 34, of which 14 were waited for; matrix products, arithmetic and copies ran while one was open for 24% of the time, Pallas kernels for 0%

profile of v1, /device:TPU:0, one launch (start us, length us, event | category | flops | bytes accessed | tf_op | source)
XLA Modules:
  0.0 369.2 jit_solution(9737610292930891844)
XLA Ops:
  0.6 7.4 %all-to-all-start.1 = ((bf16[32,344,128]{2,1,0:T(8,128)(2,1)}), bf16[32,344,128]{2,1,0:T(8,128)(2,1)}, u32[]{:S(2)}, u32[]{:S(2)}) async-start(bf16[32,344,128]{2,1,0:T(8,128)(2,1)} %bitcast.125), calls=%async_computation.1 | async-start | bytes 5636096 | tf_op jit(solution)/shard_map/all_to_all | solution.py:67
  8.1 12.6 %reshape.125 = bf16[176,4,8,344]{3,2,1,0:T(8,128)(2,1)} reshape(bf16[176,11008]{1,0:T(8,128)(2,1)} %param.6) | data formatting | bytes 7749632 | tf_op jit(solution)/shard_map/reshape | solution.py:62
  20.7 5.8 %copy.31 = bf16[4,8,176,344]{3,2,0,1:T(8,128)(2,1)} copy(bf16[4,8,176,344]{3,1,0,2:T(8,128)(2,1)} %bitcast.117) | data formatting | bytes 7749632 | tf_op jit(solution)/shard_map/transpose | solution.py:62
  26.5 4.6 %reverse_select_fusion.1 = bf16[2,2,8,176,344]{4,3,1,0,2:T(8,128)(2,1)S(1)} fusion(bf16[2,2,8,176,344]{4,3,1,0,2:T(8,128)(2,1)} %bitcast.119, pred[]{:T(512)S(6)} %eq.9), kind=kLoop, calls=%fused_computation.10 | loop fusion | flops 1937408 | bytes 7749633 | tf_op jit(solution)/shard_map/jit(_where)/select_n | solution.py:27
  31.2 2.9 reverse_select_fusion
  34.0 38.4 %all-to-all-done.1 = bf16[32,344,128]{2,1,0:T(8,128)(2,1)} async-done(((bf16[32,344,128]{2,1,0:T(8,128)(2,1)}), bf16[32,344,128]{2,1,0:T(8,128)(2,1)}, u32[]{:S(2)}, u32[]{:S(2)}) %all-to-all-start.1) | async-done | bytes 2818080 | tf_op jit(solution)/shard_map/all_to_all | solution.py:67
  72.5 4.9 %all-to-all-start = ((bf16[8,4,176,344]{3,2,1,0:T(8,128)(2,1)}), bf16[8,4,176,344]{3,2,1,0:T(8,128)(2,1)}, u32[]{:S(2)}, u32[]{:S(2)}) async-start(bf16[8,4,176,344]{3,2,1,0:T(8,128)(2,1)} %bitcast.118), calls=%async_computation | async-start | bytes 8650752 | tf_op jit(solution)/shard_map/all_to_all | solution.py:65
  77.4 7.4 %fusion.5 = f32[1024,344]{0,1:T(8,128)S(1)} fusion(bf16[4096,1024]{1,0:T(8,128)(2,1)} %param.10, f32[4096]{0:T(1024)S(1)} %copy-done.17, bf16[32,344,128]{2,1,0:T(8,128)(2,1)} %all-to-all-done.1), kind=kOutput, calls=%fused_computation.5 | convolution fusion | flops 2910846976 | bytes 12632064 | tf_op jit(solution)/shard_map/dot_general | solution.py:14
  84.8 7.4 %add_convert_fusion.1 = bf16[1024,344]{0,1:T(8,128)(2,1)S(1)} fusion(f32[1024,344]{0,1:T(8,128)S(1)} %fusion.5, bf16[4096,1024]{1,0:T(8,128)(2,1)} %param.10, f32[4096]{0:T(1024)S(1)} %copy-done.17, bf16[32,344,128]{2,1,0:T(8,128)(2,1)} %all-to-all-done.1), kind=kOutput, calls=%fused_computation.53 | convolution fusion | flops 2898968576 | bytes 13336576 | tf_op jit(solution)/shard_map/dot_general | solution.py:14
  92.2 35.5 %all-to-all-done = bf16[8,4,176,344]{3,2,1,0:T(8,128)(2,1)} async-done(((bf16[8,4,176,344]{3,2,1,0:T(8,128)(2,1)}), bf16[8,4,176,344]{3,2,1,0:T(8,128)(2,1)}, u32[]{:S(2)}, u32[]{:S(2)}) %all-to-all-start) | async-done | bytes 3874848 | tf_op jit(solution)/shard_map/all_to_all | solution.py:65
  127.7 2.6 fusion.58
  130.5 1.9 collective-permute-start.2
  134.1 1.7 fusion.71
  135.8 39.7 %collective-permute-done.1 = bf16[344,1024]{1,0:T(8,128)(2,1)S(1)} collective-permute-done((bf16[344,1024]{1,0:T(8,128)(2,1)S(1)}, bf16[344,1024]{1,0:T(8,128)(2,1)S(1)}, u32[]{:S(2)}, u32[]{:S(2)}) %collective-permute-start.1) | collective-permute-done | bytes 704544 | tf_op jit(solution)/shard_map/ppermute | solution.py:21
  175.4 1.7 fusion.72
  177.1 4.0 %add_convert_fusion = bf16[1408,1024]{1,0:T(8,128)(2,1)} fusion(f32[1408,1024]{1,0:T(8,128)S(1)} %fusion.72, f32[1408,1024]{1,0:T(8,128)S(1)} %fusion.70, f32[1408,1024]{1,0:T(8,128)S(1)} %fusion.71, bf16[1408,344]{1,0:T(8,128)(2,1)S(1)} %bitcast.124, bf16[344,1024]{1,0:T(8,128)(2,1)S(1)} %collective-permute-done.2), kind=kOutput, calls=%fused_computation.12 | convolution fusion | flops 997720064 | bytes 21858304 | tf_op jit(solution)/shard_map/dot_general | solution.py:14
  181.1 5.1 %all-to-all-start.2 = ((bf16[8,176,1024]{2,1,0:T(8,128)(2,1)}), bf16[8,176,1024]{2,1,0:T(8,128)(2,1)}, u32[]{:S(2)}, u32[]{:S(2)}) async-start(bf16[8,176,1024]{2,1,0:T(8,128)(2,1)} %bitcast.120), calls=%async_computation.2 | async-start | bytes 5767168 | tf_op jit(solution)/shard_map/all_to_all | solution.py:83
  186.8 34.7 %all-to-all-done.2 = bf16[8,176,1024]{2,1,0:T(8,128)(2,1)} async-done(((bf16[8,176,1024]{2,1,0:T(8,128)(2,1)}), bf16[8,176,1024]{2,1,0:T(8,128)(2,1)}, u32[]{:S(2)}, u32[]{:S(2)}) %all-to-all-start.2) | async-done | bytes 2883616 | tf_op jit(solution)/shard_map/all_to_all | solution.py:83
  221.4 2.4 convert_reduce_fusion
  223.9 5.5 %multiply_reduce_fusion.4 = (f32[176]{0:T(256)S(1)}, f32[176,1024]{1,0:T(8,128)S(1)}) fusion(f32[176,1024]{1,0:T(8,128)S(1)} %convert_reduce_fusion, bf16[176,4096]{1,0:T(8,128)(2,1)S(1)} %copy-done, bf16[4096,1024]{1,0:T(8,128)(2,1)} %param.10, f32[4096]{0:T(1024)S(1)} %copy-done.17), kind=kOutput, calls=%fused_computation.57 | convolution fusion | flops 1489518464 | bytes 11289280 | tf_op jit(solution)/shard_map/dot_general | solution.py:14
  232.6 14.0 %collective-permute-start.8 = (bf16[176,1024]{1,0:T(8,128)(2,1)S(1)}, bf16[176,1024]{1,0:T(8,128)(2,1)S(1)}, u32[]{:S(2)}, u32[]{:S(2)}) collective-permute-start(bf16[176,1024]{1,0:T(8,128)(2,1)S(1)} %multiply_convert_fusion), channel_id=1, source_target_pairs={{0,8},{1,9},{2,10},{3,11},{4,12},{5,13},{6,14},{7,15},{8,0},{9,1},... | collective-permute-start | bytes 1081352 | tf_op jit(solution)/shard_map/ppermute | solution.py:21
  247.7 2.0 collective-permute-start.18
  250.6 2.1 collective-permute-start.6
  255.5 2.7 collective-permute-start.9
  258.2 6.9 %collective-permute-done.18 = bf16[176,1024]{1,0:T(8,128)(2,1)S(1)} collective-permute-done((bf16[176,1024]{1,0:T(8,128)(2,1)S(1)}, bf16[176,1024]{1,0:T(8,128)(2,1)S(1)}, u32[]{:S(2)}, u32[]{:S(2)}) %collective-permute-start.18) | collective-permute-done | bytes 360480 | tf_op jit(solution)/shard_map/ppermute | solution.py:21
  265.9 13.6 %collective-permute-done.13 = bf16[176,1024]{1,0:T(8,128)(2,1)S(1)} collective-permute-done((bf16[176,1024]{1,0:T(8,128)(2,1)S(1)}, bf16[176,1024]{1,0:T(8,128)(2,1)S(1)}, u32[]{:S(2)}, u32[]{:S(2)}) %collective-permute-start.13) | collective-permute-done | bytes 360480 | tf_op jit(solution)/shard_map/ppermute | solution.py:21
  279.5 1.7 collective-permute-start.21
  283.6 1.8 multiply_reduce_fusion.3
  287.8 1.7 collective-permute-start.14
  290.3 1.7 collective-permute-start.10
  293.3 1.8 collective-permute-start.22
  298.6 2.6 collective-permute-done.10
  301.2 2.5 collective-permute-start.15
  303.7 1.8 constant_dynamic-update-slice_fusion.11
  307.6 3.1 multiply_reduce_fusion.2
  314.6 3.1 multiply_reduce_fusion
  321.2 1.7 constant_dynamic-update-slice_fusion.14
  323.0 4.0 %multiply_reduce_fusion.1 = (f32[704]{0:T(1024)S(1)}, f32[704,1024]{1,0:T(8,128)S(1)}) fusion(bf16[704,1024]{1,0:T(8,128)(2,1)} %constant_dynamic-update-slice_fusion.14, bf16[1024,1024]{1,0:T(8,128)(2,1)} %constant_dynamic-update-slice_fusion.6), kind=kOutput, calls=%fused_computation.35 | convolution fusion | flops 1477836032 | bytes 6425344 | tf_op jit(solution)/shard_map/dot_general | solution.py:93
  330.3 3.1 collective-permute-start.25
  335.4 2.5 collective-permute-start.27
  337.9 1.9 collective-permute-start.28
  340.1 3.4 collective-permute-done.28
  344.0 2.5 fusion.13
  346.7 5.3 %fusion.26 = f32[1024,1024]{1,0:T(8,128)} fusion(bf16[704,1024]{1,0:T(8,128)(2,1)} %constant_dynamic-update-slice_fusion.8, f32[704,1024]{1,0:T(8,128)S(1)} %copy-done.7, f32[704]{0:T(1024)S(1)} %sub.107), kind=kOutput, calls=%fused_computation.43 | convolution fusion | flops 1478557696 | bytes 8522496 | tf_op jit(solution)/shard_map/dot_general | solution.py:113
  352.5 4.3 %fusion.28 = f32[1024,1024]{1,0:T(8,128)S(1)} fusion(bf16[704,1024]{1,0:T(8,128)(2,1)} %copy-done.16, f32[704,1024]{1,0:T(8,128)} %copy-done.4, f32[704]{0:T(1024)S(1)} %sub.104), kind=kOutput, calls=%fused_computation.44 | convolution fusion | flops 1478557696 | bytes 8522496 | tf_op jit(solution)/shard_map/dot_general | solution.py:113
  356.9 2.0 fusion.24
  359.1 3.9 %add_add_fusion = f32[1024,1024]{1,0:T(8,128)S(1)} fusion(f32[1024,1024]{1,0:T(8,128)S(1)} %fusion.24, f32[1024,1024]{1,0:T(8,128)S(1)} %fusion.28, f32[1024,1024]{1,0:T(8,128)S(1)} %copy-done.10, bf16[704,1024]{1,0:T(8,128)(2,1)} %constant_dynamic-update-slice_fusion.20, f32[704,1024]{1,0:T(8,128)S(1)} %get-tuple-element.41, f32[704]{0:T(1024)S(1)} %sub.113), kind=kOutput, calls=%fused_computation.13 | convolution fusion | flops 1481703424 | bytes 21105408 | tf_op jit(solution)/shard_map/dot_general | solution.py:113
  367.3 1.7 fusion.21
  (183 shorter events, 42.0 us)
Async XLA Ops:
  0.6 223.2 %copy-start = (bf16[176,4096]{1,0:T(8,128)(2,1)S(1)}, bf16[176,4096]{1,0:T(8,128)(2,1)}, u32[]{:S(2)}) copy-start(bf16[176,4096]{1,0:T(8,128)(2,1)} %param.7) | copy-start | bytes 4325380
  0.6 71.8 %all-to-all-start.1 = ((bf16[32,344,128]{2,1,0:T(8,128)(2,1)}), bf16[32,344,128]{2,1,0:T(8,128)(2,1)}, u32[]{:S(2)}, u32[]{:S(2)}) async-start(bf16[32,344,128]{2,1,0:T(8,128)(2,1)} %bitcast.125), calls=%async_computation.1 | async-start | bytes 5636096 | tf_op jit(solution)/shard_map/all_to_all | solution.py:67
  72.5 4.9 %copy-start.17 = (f32[4096]{0:T(1024)S(1)}, f32[4096]{0:T(1024)}, u32[]{:S(2)}) copy-start(f32[4096]{0:T(1024)} %param.9) | copy-start | bytes 49156
  72.5 55.3 %all-to-all-start = ((bf16[8,4,176,344]{3,2,1,0:T(8,128)(2,1)}), bf16[8,4,176,344]{3,2,1,0:T(8,128)(2,1)}, u32[]{:S(2)}, u32[]{:S(2)}) async-start(bf16[8,4,176,344]{3,2,1,0:T(8,128)(2,1)} %bitcast.118), calls=%async_computation | async-start | bytes 8650752 | tf_op jit(solution)/shard_map/all_to_all | solution.py:65
  92.2 41.9 %collective-permute-start = (bf16[344,1024]{1,0:T(8,128)(2,1)S(1)}, bf16[344,1024]{1,0:T(8,128)(2,1)S(1)}, u32[]{:S(2)}, u32[]{:S(2)}) collective-permute-start(bf16[344,1024]{1,0:T(8,128)(2,1)S(1)} %bitcast.126), channel_id=1, source_target_pairs={{0,8},{1,9},{2,10},{3,11},{4,12},{5,13},{6,14},{7,15},{8,0},{9,1},... | collective-permute-start | bytes 2113544 | tf_op jit(solution)/shard_map/ppermute | solution.py:21
  130.4 45.0 %collective-permute-start.1 = (bf16[344,1024]{1,0:T(8,128)(2,1)S(1)}, bf16[344,1024]{1,0:T(8,128)(2,1)S(1)}, u32[]{:S(2)}, u32[]{:S(2)}) collective-permute-start(bf16[344,1024]{1,0:T(8,128)(2,1)S(1)} %bitcast.127), channel_id=1, source_target_pairs={{0,16},{1,17},{2,18},{3,19},{4,20},{5,21},{6,22},{7,23},{8,24},{9,... | collective-permute-start | bytes 2113544 | tf_op jit(solution)/shard_map/ppermute | solution.py:21
  130.5 46.6 %collective-permute-start.2 = (bf16[344,1024]{1,0:T(8,128)(2,1)S(1)}, bf16[344,1024]{1,0:T(8,128)(2,1)S(1)}, u32[]{:S(2)}, u32[]{:S(2)}) collective-permute-start(bf16[344,1024]{1,0:T(8,128)(2,1)S(1)} %bitcast.128), channel_id=1, source_target_pairs={{0,24},{1,25},{2,26},{3,27},{4,28},{5,29},{6,30},{7,31},{8,16},{9,... | collective-permute-start | bytes 2113544 | tf_op jit(solution)/shard_map/ppermute | solution.py:21
  181.1 5.1 %copy-start.11 = (bf16[512,1024]{1,0:T(8,128)(2,1)S(1)}, bf16[512,1024]{1,0:T(8,128)(2,1)}, u32[]{:S(2)}) copy-start(bf16[512,1024]{1,0:T(8,128)(2,1)} %param.11) | copy-start | bytes 3145732
  181.1 40.3 %all-to-all-start.2 = ((bf16[8,176,1024]{2,1,0:T(8,128)(2,1)}), bf16[8,176,1024]{2,1,0:T(8,128)(2,1)}, u32[]{:S(2)}, u32[]{:S(2)}) async-start(bf16[8,176,1024]{2,1,0:T(8,128)(2,1)} %bitcast.120), calls=%async_computation.2 | async-start | bytes 5767168 | tf_op jit(solution)/shard_map/all_to_all | solution.py:83
  186.2 60.4 %collective-permute-start.7 = (bf16[512,1024]{1,0:T(8,128)(2,1)S(1)}, bf16[512,1024]{1,0:T(8,128)(2,1)S(1)}, u32[]{:S(2)}, u32[]{:S(2)}) collective-permute-start(bf16[512,1024]{1,0:T(8,128)(2,1)S(1)} %copy-done.11), channel_id=1, source_target_pairs={{0,1},{1,0},{2,3},{3,2},{4,5},{5,4},{6,7},{7,6},{8,9},{9,8},{10,11... | collective-permute-start | bytes 3145736 | tf_op jit(solution)/shard_map/ppermute | solution.py:21
  230.2 19.4 %collective-permute-start.5 = (bf16[88,1024]{1,0:T(8,128)(2,1)S(1)}, bf16[88,1024]{1,0:T(8,128)(2,1)}, u32[]{:S(2)}, u32[]{:S(2)}) collective-permute-start(bf16[88,1024]{1,0:T(8,128)(2,1)S(1)} %get-tuple-element.6), channel_id=1, source_target_pairs={{0,4},{1,5},{2,6},{3,7},{4,0},{5,1},{6,2},{7,3},{8,12},{9,13},{10,... | collective-permute-start | bytes 540680 | tf_op jit(solution)/shard_map/ppermute | solution.py:21
  232.6 20.7 %copy-start.15 = (bf16[704,1024]{1,0:T(8,128)(2,1)S(1)}, bf16[704,1024]{1,0:T(8,128)(2,1)}, u32[]{:S(2)}) copy-start(bf16[704,1024]{1,0:T(8,128)(2,1)} %get-tuple-element.7) | copy-start | bytes 4325380
  232.6 22.2 %collective-permute-start.8 = (bf16[176,1024]{1,0:T(8,128)(2,1)S(1)}, bf16[176,1024]{1,0:T(8,128)(2,1)S(1)}, u32[]{:S(2)}, u32[]{:S(2)}) collective-permute-start(bf16[176,1024]{1,0:T(8,128)(2,1)S(1)} %multiply_convert_fusion), channel_id=1, source_target_pairs={{0,8},{1,9},{2,10},{3,11},{4,12},{5,13},{6,14},{7,15},{8,0},{9,1},... | collective-permute-start | bytes 1081352 | tf_op jit(solution)/shard_map/ppermute | solution.py:21
  246.6 6.1 %collective-permute-start.3 = (bf16[88,1024]{1,0:T(8,128)(2,1)S(1)}, bf16[88,1024]{1,0:T(8,128)(2,1)S(1)}, u32[]{:S(2)}, u32[]{:S(2)}) collective-permute-start(bf16[88,1024]{1,0:T(8,128)(2,1)S(1)} %get-tuple-element.8), channel_id=1, source_target_pairs={{0,2},{1,3},{2,0},{3,1},{4,6},{5,7},{6,4},{7,5},{8,10},{9,11},{10,... | collective-permute-start | bytes 540680 | tf_op jit(solution)/shard_map/ppermute | solution.py:21
  247.7 17.5 %collective-permute-start.18 = (bf16[176,1024]{1,0:T(8,128)(2,1)S(1)}, bf16[176,1024]{1,0:T(8,128)(2,1)S(1)}, u32[]{:S(2)}, u32[]{:S(2)}) collective-permute-start(bf16[176,1024]{1,0:T(8,128)(2,1)S(1)} %multiply_convert_fusion), channel_id=1, source_target_pairs={{0,24},{1,25},{2,26},{3,27},{4,28},{5,29},{6,30},{7,31},{8,16},{9,... | collective-permute-start | bytes 1081352 | tf_op jit(solution)/shard_map/ppermute | solution.py:21
  249.6 29.8 %collective-permute-start.13 = (bf16[176,1024]{1,0:T(8,128)(2,1)S(1)}, bf16[176,1024]{1,0:T(8,128)(2,1)S(1)}, u32[]{:S(2)}, u32[]{:S(2)}) collective-permute-start(bf16[176,1024]{1,0:T(8,128)(2,1)S(1)} %multiply_convert_fusion), channel_id=1, source_target_pairs={{0,16},{1,17},{2,18},{3,19},{4,20},{5,21},{6,22},{7,23},{8,24},{9,... | collective-permute-start | bytes 1081352 | tf_op jit(solution)/shard_map/ppermute | solution.py:21
  250.6 33.1 %copy-start.12 = (bf16[1024,1024]{1,0:T(8,128)(2,1)S(1)}, bf16[1024,1024]{1,0:T(8,128)(2,1)}, u32[]{:S(2)}) copy-start(bf16[1024,1024]{1,0:T(8,128)(2,1)} %constant_dynamic-update-slice_fusion.6) | copy-start | bytes 6291460
  250.6 32.6 %collective-permute-start.6 = (bf16[176,1024]{1,0:T(8,128)(2,1)S(1)}, bf16[176,1024]{1,0:T(8,128)(2,1)S(1)}, u32[]{:S(2)}, u32[]{:S(2)}) collective-permute-start(bf16[176,1024]{1,0:T(8,128)(2,1)S(1)} %pad_maximum_fusion.1), channel_id=1, source_target_pairs={{0,2},{1,3},{2,0},{3,1},{4,6},{5,7},{6,4},{7,5},{8,10},{9,11},{10,... | collective-permute-start | bytes 1081352 | tf_op jit(solution)/shard_map/ppermute | solution.py:21
  252.7 29.2 %collective-permute-start.4 = (bf16[176,1024]{1,0:T(8,128)(2,1)S(1)}, bf16[176,1024]{1,0:T(8,128)(2,1)S(1)}, u32[]{:S(2)}, u32[]{:S(2)}) collective-permute-start(bf16[176,1024]{1,0:T(8,128)(2,1)S(1)} %pad_maximum_fusion), channel_id=1, source_target_pairs={{0,4},{1,5},{2,6},{3,7},{4,0},{5,1},{6,2},{7,3},{8,12},{9,13},{10,... | collective-permute-start | bytes 1081352 | tf_op jit(solution)/shard_map/ppermute | solution.py:21
  255.5 32.3 %collective-permute-start.9 = (bf16[88,1024]{1,0:T(8,128)(2,1)S(1)}, bf16[88,1024]{1,0:T(8,128)(2,1)S(1)}, u32[]{:S(2)}, u32[]{:S(2)}) collective-permute-start(bf16[88,1024]{1,0:T(8,128)(2,1)S(1)} %get-tuple-element.11), channel_id=1, source_target_pairs={{0,2},{1,3},{2,0},{3,1},{4,6},{5,7},{6,4},{7,5},{8,10},{9,11},{10,... | collective-permute-start | bytes 540680 | tf_op jit(solution)/shard_map/ppermute | solution.py:21
  265.1 25.2 %collective-permute-start.11 = (bf16[88,1024]{1,0:T(8,128)(2,1)S(1)}, bf16[88,1024]{1,0:T(8,128)(2,1)S(1)}, u32[]{:S(2)}, u32[]{:S(2)}) collective-permute-start(bf16[88,1024]{1,0:T(8,128)(2,1)S(1)} %get-tuple-element.9), channel_id=1, source_target_pairs={{0,4},{1,5},{2,6},{3,7},{4,0},{5,1},{6,2},{7,3},{8,12},{9,13},{10,... | collective-permute-start | bytes 540680 | tf_op jit(solution)/shard_map/ppermute | solution.py:21
  279.5 13.5 %collective-permute-start.21 = (bf16[88,1024]{1,0:T(8,128)(2,1)S(1)}, bf16[88,1024]{1,0:T(8,128)(2,1)S(1)}, u32[]{:S(2)}, u32[]{:S(2)}) collective-permute-start(bf16[88,1024]{1,0:T(8,128)(2,1)S(1)} %get-tuple-element.12), channel_id=1, source_target_pairs={{0,4},{1,5},{2,6},{3,7},{4,0},{5,1},{6,2},{7,3},{8,12},{9,13},{10,... | collective-permute-start | bytes 540680 | tf_op jit(solution)/shard_map/ppermute | solution.py:21
  281.9 11.4 %collective-permute-start.19 = (bf16[88,1024]{1,0:T(8,128)(2,1)S(1)}, bf16[88,1024]{1,0:T(8,128)(2,1)S(1)}, u32[]{:S(2)}, u32[]{:S(2)}) collective-permute-start(bf16[88,1024]{1,0:T(8,128)(2,1)S(1)} %get-tuple-element.14), channel_id=1, source_target_pairs={{0,2},{1,3},{2,0},{3,1},{4,6},{5,7},{6,4},{7,5},{8,10},{9,11},{10,... | collective-permute-start | bytes 540680 | tf_op jit(solution)/shard_map/ppermute | solution.py:21
  283.2 13.4 %collective-permute-start.16 = (bf16[88,1024]{1,0:T(8,128)(2,1)S(1)}, bf16[88,1024]{1,0:T(8,128)(2,1)S(1)}, u32[]{:S(2)}, u32[]{:S(2)}) collective-permute-start(bf16[88,1024]{1,0:T(8,128)(2,1)S(1)} %get-tuple-element.15), channel_id=1, source_target_pairs={{0,4},{1,5},{2,6},{3,7},{4,0},{5,1},{6,2},{7,3},{8,12},{9,13},{10,... | collective-permute-start | bytes 540680 | tf_op jit(solution)/shard_map/ppermute | solution.py:21
  287.8 9.8 %collective-permute-start.14 = (bf16[88,1024]{1,0:T(8,128)(2,1)S(1)}, bf16[88,1024]{1,0:T(8,128)(2,1)S(1)}, u32[]{:S(2)}, u32[]{:S(2)}) collective-permute-start(bf16[88,1024]{1,0:T(8,128)(2,1)S(1)} %get-tuple-element.17), channel_id=1, source_target_pairs={{0,2},{1,3},{2,0},{3,1},{4,6},{5,7},{6,4},{7,5},{8,10},{9,11},{10,... | collective-permute-start | bytes 540680 | tf_op jit(solution)/shard_map/ppermute | solution.py:21
  290.3 10.9 %collective-permute-start.10 = (bf16[176,1024]{1,0:T(8,128)(2,1)}, bf16[176,1024]{1,0:T(8,128)(2,1)}, u32[]{:S(2)}, u32[]{:S(2)}) collective-permute-start(bf16[176,1024]{1,0:T(8,128)(2,1)} %pad_maximum_fusion.2), channel_id=1, source_target_pairs={{0,4},{1,5},{2,6},{3,7},{4,0},{5,1},{6,2},{7,3},{8,12},{9,13},{10,... | collective-permute-start | bytes 1081352 | tf_op jit(solution)/shard_map/ppermute | solution.py:21
  293.0 13.9 %collective-permute-start.12 = (bf16[176,1024]{1,0:T(8,128)(2,1)}, bf16[176,1024]{1,0:T(8,128)(2,1)S(1)}, u32[]{:S(2)}, u32[]{:S(2)}) collective-permute-start(bf16[176,1024]{1,0:T(8,128)(2,1)} %pad_maximum_fusion.3), channel_id=1, source_target_pairs={{0,2},{1,3},{2,0},{3,1},{4,6},{5,7},{6,4},{7,5},{8,10},{9,11},{10,... | collective-permute-start | bytes 1081352 | tf_op jit(solution)/shard_map/ppermute | solution.py:21
  293.3 14.3 %copy-start.13 = (bf16[1024,1024]{1,0:T(8,128)(2,1)S(1)}, bf16[1024,1024]{1,0:T(8,128)(2,1)}, u32[]{:S(2)}) copy-start(bf16[1024,1024]{1,0:T(8,128)(2,1)} %constant_dynamic-update-slice_fusion.6) | copy-start | bytes 6291460
  293.3 20.5 %collective-permute-start.22 = (bf16[176,1024]{1,0:T(8,128)(2,1)S(1)}, bf16[176,1024]{1,0:T(8,128)(2,1)S(1)}, u32[]{:S(2)}, u32[]{:S(2)}) collective-permute-start(bf16[176,1024]{1,0:T(8,128)(2,1)S(1)} %pad_maximum_fusion.7), channel_id=1, source_target_pairs={{0,2},{1,3},{2,0},{3,1},{4,6},{5,7},{6,4},{7,5},{8,10},{9,11},{10,... | collective-permute-start | bytes 1081352 | tf_op jit(solution)/shard_map/ppermute | solution.py:21
  296.6 14.9 %collective-permute-start.20 = (bf16[176,1024]{1,0:T(8,128)(2,1)S(1)}, bf16[176,1024]{1,0:T(8,128)(2,1)S(1)}, u32[]{:S(2)}, u32[]{:S(2)}) collective-permute-start(bf16[176,1024]{1,0:T(8,128)(2,1)S(1)} %pad_maximum_fusion.6), channel_id=1, source_target_pairs={{0,4},{1,5},{2,6},{3,7},{4,0},{5,1},{6,2},{7,3},{8,12},{9,13},{10,... | collective-permute-start | bytes 1081352 | tf_op jit(solution)/shard_map/ppermute | solution.py:21
  297.6 23.6 %collective-permute-start.17 = (bf16[176,1024]{1,0:T(8,128)(2,1)}, bf16[176,1024]{1,0:T(8,128)(2,1)}, u32[]{:S(2)}, u32[]{:S(2)}) collective-permute-start(bf16[176,1024]{1,0:T(8,128)(2,1)} %pad_maximum_fusion.5), channel_id=1, source_target_pairs={{0,2},{1,3},{2,0},{3,1},{4,6},{5,7},{6,4},{7,5},{8,10},{9,11},{10,... | collective-permute-start | bytes 1081352 | tf_op jit(solution)/shard_map/ppermute | solution.py:21
  301.2 17.4 %collective-permute-start.15 = (bf16[176,1024]{1,0:T(8,128)(2,1)S(1)}, bf16[176,1024]{1,0:T(8,128)(2,1)S(1)}, u32[]{:S(2)}, u32[]{:S(2)}) collective-permute-start(bf16[176,1024]{1,0:T(8,128)(2,1)S(1)} %pad_maximum_fusion.4), channel_id=1, source_target_pairs={{0,4},{1,5},{2,6},{3,7},{4,0},{5,1},{6,2},{7,3},{8,12},{9,13},{10,... | collective-permute-start | bytes 1081352 | tf_op jit(solution)/shard_map/ppermute | solution.py:21
  310.8 7.0 %copy-start.6 = (f32[704,1024]{1,0:T(8,128)}, f32[704,1024]{1,0:T(8,128)S(1)}, u32[]{:S(2)}) copy-start(f32[704,1024]{1,0:T(8,128)S(1)} %get-tuple-element.45) | copy-start | bytes 8650756
  317.8 41.1 %copy-start.2 = (f32[704,1024]{1,0:T(8,128)}, f32[704,1024]{1,0:T(8,128)S(1)}, u32[]{:S(2)}) copy-start(f32[704,1024]{1,0:T(8,128)S(1)} %get-tuple-element.41) | copy-start | bytes 8650756
  329.9 3.8 %collective-permute-start.23 = (f32[2,2,2,2,176]{4,3,2,1,0:T(2,128)S(1)}, f32[2,2,2,2,176]{4,3,2,1,0:T(2,128)S(1)}, u32[]{:S(2)}, u32[]{:S(2)}) collective-permute-start(f32[2,2,2,2,176]{4,3,2,1,0:T(2,128)S(1)} %broadcast_select_fusion.1), channel_id=1, source_target_pairs={{0,2},{1,3},{2,0},{3,1},{4,6},{5,7},{6,4},{7,5},{8,10},{9,11},{10,... | collective-permute-start | bytes 33800 | tf_op jit(solution)/shard_map/ppermute | solution.py:21
  330.2 3.7 %collective-permute-start.24 = (f32[2,2,2,2,176]{4,3,2,1,0:T(2,128)S(1)}, f32[2,2,2,2,176]{4,3,2,1,0:T(2,128)S(1)}, u32[]{:S(2)}, u32[]{:S(2)}) collective-permute-start(f32[2,2,2,2,176]{4,3,2,1,0:T(2,128)S(1)} %broadcast_select_fusion.1), channel_id=1, source_target_pairs={{0,4},{1,5},{2,6},{3,7},{4,0},{5,1},{6,2},{7,3},{8,12},{9,13},{10,... | collective-permute-start | bytes 33800 | tf_op jit(solution)/shard_map/ppermute | solution.py:21
  330.3 4.8 %collective-permute-start.25 = (f32[2,2,2,2,176]{4,3,2,1,0:T(2,128)S(1)}, f32[2,2,2,2,176]{4,3,2,1,0:T(2,128)S(1)}, u32[]{:S(2)}, u32[]{:S(2)}) collective-permute-start(f32[2,2,2,2,176]{4,3,2,1,0:T(2,128)S(1)} %broadcast_select_fusion.1), channel_id=1, source_target_pairs={{0,6},{1,7},{2,4},{3,5},{4,2},{5,3},{6,0},{7,1},{8,14},{9,15},{10,... | collective-permute-start | bytes 33800 | tf_op jit(solution)/shard_map/ppermute | solution.py:21
  335.3 4.5 %collective-permute-start.26 = (f32[2,2,2,2,176]{4,3,2,1,0:T(2,128)S(1)}, f32[2,2,2,2,176]{4,3,2,1,0:T(2,128)S(1)}, u32[]{:S(2)}, u32[]{:S(2)}) collective-permute-start(f32[2,2,2,2,176]{4,3,2,1,0:T(2,128)S(1)} %log_add_fusion.1), channel_id=1, source_target_pairs={{0,8},{1,9},{2,10},{3,11},{4,12},{5,13},{6,14},{7,15},{8,0},{9,1},... | collective-permute-start | bytes 33800 | tf_op jit(solution)/shard_map/ppermute | solution.py:21
  335.4 4.7 %collective-permute-start.27 = (f32[2,2,2,2,176]{4,3,2,1,0:T(2,128)S(1)}, f32[2,2,2,2,176]{4,3,2,1,0:T(2,128)S(1)}, u32[]{:S(2)}, u32[]{:S(2)}) collective-permute-start(f32[2,2,2,2,176]{4,3,2,1,0:T(2,128)S(1)} %log_add_fusion.1), channel_id=1, source_target_pairs={{0,16},{1,17},{2,18},{3,19},{4,20},{5,21},{6,22},{7,23},{8,24},{9,... | collective-permute-start | bytes 33800 | tf_op jit(solution)/shard_map/ppermute | solution.py:21
  337.9 5.5 %collective-permute-start.28 = (f32[2,2,2,2,176]{4,3,2,1,0:T(2,128)S(1)}, f32[2,2,2,2,176]{4,3,2,1,0:T(2,128)S(1)}, u32[]{:S(2)}, u32[]{:S(2)}) collective-permute-start(f32[2,2,2,2,176]{4,3,2,1,0:T(2,128)S(1)} %log_add_fusion.1), channel_id=1, source_target_pairs={{0,24},{1,25},{2,26},{3,27},{4,28},{5,29},{6,30},{7,31},{8,16},{9,... | collective-permute-start | bytes 33800 | tf_op jit(solution)/shard_map/ppermute | solution.py:21
  344.0 2.7 copy-start.7
  352.5 4.4 %copy-start.9 = (f32[704,1024]{1,0:T(8,128)S(1)}, f32[704,1024]{1,0:T(8,128)}, u32[]{:S(2)}) copy-start(f32[704,1024]{1,0:T(8,128)} %copy-done.8) | copy-start | bytes 8650756
  352.5 4.4 %copy-start.14 = (bf16[704,1024]{1,0:T(8,128)(2,1)S(1)}, bf16[704,1024]{1,0:T(8,128)(2,1)}, u32[]{:S(2)}) copy-start(bf16[704,1024]{1,0:T(8,128)(2,1)} %constant_dynamic-update-slice_fusion.14) | copy-start | bytes 4325380
  356.9 2.2 copy-start.10
  359.1 4.1 %copy-start.5 = (f32[704,1024]{1,0:T(8,128)S(1)}, f32[704,1024]{1,0:T(8,128)}, u32[]{:S(2)}) copy-start(f32[704,1024]{1,0:T(8,128)} %copy-done.4) | copy-start | bytes 8650756
  363.1 4.2 %collective-permute-start.29 = (bf16[512,1024]{1,0:T(8,128)(2,1)S(1)}, bf16[512,1024]{1,0:T(8,128)(2,1)S(1)}, u32[]{:S(2)}, u32[]{:S(2)}) collective-permute-start(bf16[512,1024]{1,0:T(8,128)(2,1)S(1)} %slice.241), channel_id=1, source_target_pairs={{0,1},{1,0},{2,3},{3,2},{4,5},{5,4},{6,7},{7,6},{8,9},{9,8},{10,11... | collective-permute-start | bytes 3145736 | tf_op jit(solution)/shard_map/ppermute | solution.py:21
  364.9 4.1 %copy-start.1 = (bf16[176,4096]{1,0:T(8,128)(2,1)S(1)}, bf16[176,4096]{1,0:T(8,128)(2,1)}, u32[]{:S(2)}) copy-start(bf16[176,4096]{1,0:T(8,128)(2,1)} %param.7) | copy-start | bytes 4325380
  365.5 1.2 collective-permute-start.30
  (4 other events, 6.8 us)

commit v2 on v0

v2 whole, which is shorter than its diff:
```python
import math

import jax
import jax.numpy as jnp
from jax import lax
from jax.experimental import pallas as pl
from jax.experimental.pallas import tpu as pltpu
from jax.sharding import PartitionSpec as P


F32 = jnp.float32
BF16 = jnp.bfloat16
PLANE = 8
QUAD = 4


def dot(a, b):
    return jnp.dot(a, b, preferred_element_type=F32)


def after(v, *others):
    return lax.optimization_barrier((v, *others))[0]


def lse(parts):
    top = parts[0]
    for p in parts[1:]:
        top = jnp.maximum(top, p)
    return top + jnp.log(sum(jnp.exp(p - top) for p in parts))


def weigh_kernel(count, *refs):
    scores, totals, blocks = refs[:count], refs[count : 2 * count], refs[2 * count : 3 * count]
    weighted, counts = refs[3 * count :]
    sums, masses = 0.0, 0.0
    for s, t, b in zip(scores, totals, blocks):
        prob = jnp.exp(s[...] - t[...])
        masses = masses + jnp.sum(prob, axis=1, keepdims=True)
        sums = sums + dot(prob.astype(BF16), b[...])
    weighted[...] = sums.astype(weighted.dtype)
    counts[...] = masses


def weigh(scores, totals, blocks, start, size, dtype, scale):
    count = len(scores)
    width = blocks[0].shape[1]
    tile = math.gcd(size, 256)
    first = start // tile
    passages = count * blocks[0].shape[0]
    whole = lambda a: pl.BlockSpec(a.shape, lambda i: (0, 0))
    return pl.pallas_call(
        lambda *refs: weigh_kernel(count, *refs),
        grid=(size // tile,),
        in_specs=[pl.BlockSpec((tile, s.shape[1]), lambda i: (first + i, 0)) for s in scores]
        + [whole(t) for t in totals]
        + [whole(b) for b in blocks],
        out_specs=[pl.BlockSpec((tile, width), lambda i: (i, 0)), pl.BlockSpec((tile, 1), lambda i: (i, 0))],
        out_shape=[jax.ShapeDtypeStruct((size, width), dtype), jax.ShapeDtypeStruct((size, 1), F32)],
        compiler_params=pltpu.CompilerParams(vmem_limit_bytes=48 * 2**20),
        cost_estimate=pl.CostEstimate(
            flops=2 * passages * size * width,
            bytes_accessed=passages * (4 * size + 2 * width) + 4 * size * width,
            transcendentals=passages * size,
        ),
    )(*scores, *totals, *blocks)


def deal_kernel(position, hidden, blocks):
    share = blocks.shape[2]
    for d in range(blocks.shape[0]):
        blocks[position[d]] = hidden[:, d * share : (d + 1) * share]


def deal(hidden, position):
    rows, hid = hidden.shape
    n = position.shape[0]
    vmem = pl.BlockSpec(memory_space=pltpu.VMEM)
    return pl.pallas_call(
        deal_kernel,
        in_specs=[pl.BlockSpec(memory_space=pltpu.SMEM), vmem],
        out_specs=vmem,
        out_shape=jax.ShapeDtypeStruct((n, rows, hid // n), hidden.dtype),
        compiler_params=pltpu.CompilerParams(vmem_limit_bytes=32 * 2**20),
        cost_estimate=pl.CostEstimate(flops=0, bytes_accessed=4 * rows * hid, transcendentals=0),
    )(position, hidden)


def arrivals(lines):
    table = []
    for z in range(lines):
        near = [(s, w, z - s if w == 0 else z + s) for s in range(1, lines) for w in (1, 0)]
        table.append([e for e in near if 0 <= e[2] < lines])
    return table


def make_body(n, lines):
    table = arrivals(lines)

    def hop(v, k):
        return lax.ppermute(v, "dp", [(i, i ^ k) for i in range(n)])

    def up(v):
        return lax.ppermute(v, "dp", [(i, i + PLANE) for i in range(n - PLANE)])

    def down(v):
        return lax.ppermute(v, "dp", [(i + PLANE, i) for i in range(n - PLANE)])

    def choose(line, values):
        out = values[-1]
        for z in range(lines - 2, -1, -1):
            if values[z] is not out:
                out = jnp.where(line <= z, values[z], out)
        return out

    def gather(v):
        first = [v]
        for k in range(1, lines):
            first.append(hop(after(v, first[-1]) if k > 2 else v, k * PLANE))
        slots = []
        for k, s in enumerate(first):
            x, y = hop(s, 2), hop(s, 4)
            far = hop(x, 4) if k % 2 == 0 else hop(y, 2)
            slots.append(jnp.concatenate([s, x, y, far]))
        return slots

    def body(hidden, residual, down_weight, gain, proj_weight, centroids):
        me = lax.axis_index("dp")
        line, quad, core = me // PLANE, (me // 2) % QUAD, me % 2
        rows, hid = hidden.shape
        share = hid // n
        width = proj_weight.shape[1]
        cents = centroids.shape[0]

        orders = [[z] + [e[2] for e in table[z]] for z in range(lines)]
        place = jnp.array([[order.index(z) for z in range(lines)] for order in orders], jnp.int32)[line]
        d = jnp.arange(n)
        position = (((d // 2 % QUAD) ^ quad) * lines + place[d // PLANE]) * 2 + ((d % 2) ^ core)
        blocks = deal(hidden, position.astype(jnp.int32)).reshape(QUAD, lines, 2, rows, share)
        units = [blocks[0]] + [hop(blocks[k], 2 * k) for k in range(1, QUAD - 1)]

        down_rows = lax.all_to_all(down_weight, "dp", 0, 1, tiled=True)
        own = gain[:, None] * proj_weight.astype(F32)
        full = lax.all_gather(own, "cent", axis=0, tiled=True)
        high = lax.reduce_precision(full, 8, 7)
        low = (full - high).astype(BF16)
        high = high.astype(BF16)
        direct = dot(residual, own.astype(BF16))
        pair = jnp.concatenate([centroids, hop(centroids, 1)])
        down_rows, high, low, direct, pair, blocks = lax.optimization_barrier(
            (down_rows, high, low, direct, pair, blocks)
        )
        fold = (dot(down_rows, high) + dot(down_rows, low)).astype(BF16)
        fold, last = lax.optimization_barrier((fold, blocks[QUAD - 1]))
        units.append(hop(last, 2 * (QUAD - 1)))

        moved = {(0, 0): fold, (0, 1): fold}
        for s in range(1, lines):
            below, above = moved[s - 1, 0], moved[s - 1, 1]
            if s == lines - 1:
                below, above, units[-1] = lax.optimization_barrier((below, above, units[-1]))
            moved[s, 0], moved[s, 1] = up(below), down(above)
        folds = [fold]
        for s in range(lines - 1):
            folds.append(choose(line, [moved[table[z][s][:2]] for z in range(lines)]))
        units = jnp.concatenate(units, axis=2)
        part = 0.0
        for j, block in enumerate(folds):
            part = part + dot(units[j, 0], block) + dot(units[j, 1], hop(block, 1))
        part = part.reshape(QUAD, rows, width)

        raw = part[0] + direct
        for k in range(1, QUAD):
            raw = raw + hop(part[k].astype(BF16), 2 * k).astype(F32)
        raw = lax.psum(raw, "cent")
        embed = (raw * lax.rsqrt(jnp.mean(raw * raw, axis=1, keepdims=True) + 1e-06)).astype(BF16)

        inverse = 1.0 / (math.sqrt(width) * 0.05)
        slots = gather(embed)
        scores, local = [], []
        for block in slots:
            s = lax.dot_general(pair, block, (((1,), (1,)), ((), ())), preferred_element_type=F32)
            s = s * inverse
            top = jnp.max(s, axis=0, keepdims=True)
            scores.append(s)
            local.append(top + jnp.log(jnp.sum(jnp.exp(s - top), axis=0, keepdims=True)))

        v = jnp.concatenate(local).reshape(lines, QUAD, rows)
        got = [v] + [hop(v, 2 * k) for k in range(1, QUAD)]
        v = lse([jnp.stack([g[:, j ^ k] for j in range(QUAD)], axis=1) for k, g in enumerate(got)])
        got = [v] + [hop(v, PLANE * k) for k in range(1, lines)]
        v = lse([jnp.stack([g[j ^ k] for j in range(lines)]) for k, g in enumerate(got)])
        if lax.axis_size("cent") > 1:
            top = lax.pmax(v, "cent")
            v = top + jnp.log(lax.psum(jnp.exp(v - top), "cent"))
        totals = [v[k].reshape(1, QUAD * rows) for k in range(lines)]

        scale_up = cents * n * lax.axis_size("cent") / (rows * n)
        far, far_counts = weigh(scores, totals, slots, cents, cents, BF16, scale_up)
        near, near_counts = weigh(scores, totals, slots, 0, cents, F32, scale_up)
        weighted = scale_up * (near + hop(far, 1).astype(F32))
        counts = scale_up * (near_counts[:, 0] + hop(far_counts[:, 0], 1))
        return weighted, counts

    return body


def solution(mesh):
    n = mesh.shape["dp"]
    in_specs = (
        P("dp", "cent"),
        P("dp", "cent"),
        P("cent", "dp"),
        P("cent"),
        P("cent", None),
        P(("dp", "cent"), None),
    )
    out_specs = (P(("dp", "cent"), None), P(("dp", "cent")))
    return jax.shard_map(
        make_body(n, n // PLANE), mesh=mesh, in_specs=in_specs, out_specs=out_specs, check_vma=False
    )
```

time: 741 us -> 303 us (0.41)
  waiting for transfers between devices: 569 us -> 129 us
  blocking collectives: 79.8 us -> 0 us
  starting transfers between devices: 0.08 us -> 59.5 us
  local copies, waits for them, and re-layouts: 0.01 us -> 34.7 us
  matrix products: 64.6 us -> 31.6 us
  other arithmetic: 13.5 us -> 30.2 us
  Pallas kernels: 0 us -> 15.6 us
  between operations: 14.1 us -> 1.28 us
    all_gather x2 -> x0, waiting for transfers between devices: 568 us -> none  [the longest x1 479 us: body(): lax.all_gather(down_weight, 'dp', axis=1, tiled=True)]
    ppermute x0 -> x40, waiting for transfers between devices: none -> 87 us  [the longest x34 65 us: hop(): return lax.ppermute(v, 'dp', [(i, i ^ k) for i in range(n)])]
    ppermute x0 -> x40, starting transfers between devices: none -> 52.1 us  [the longest x34 36.2 us: hop(): return lax.ppermute(v, 'dp', [(i, i ^ k) for i in range(n)])]
    all_to_all x0 -> x1, waiting for transfers between devices: none -> 42.5 us  [body(): down_rows = lax.all_to_all(down_weight, 'dp', 0, 1, tiled=True)]
    psum x1 -> x0, blocking collectives: 40.8 us -> none  [body(): lax.psum(jnp.sum(jnp.exp(scores - row_max[:, None]), axis=1), ('dp', 'cen...]
    pmax x1 -> x0, blocking collectives: 39 us -> none  [body(): row_max = lax.pmax(local_max, ('dp', 'cent'))]
    dot_general x4 -> x15, matrix products: 64.6 us -> 31.6 us  [the longest x11 19.6 us: dot(): return jnp.dot(a, b, preferred_element_type=F32)]
    unnamed x2 -> x74, local copies, waits for them, and re-layouts: 0.01 us -> 22.4 us
  transfers between devices with their start and end apart: 2 -> 41, of which waited for: 2 -> 21; matrix products, arithmetic and copies ran while one was open for 0% -> 21% of each run, Pallas kernels for 0% -> 3%
where the time goes in v2:
time: 303 us; the launch traced here: 302 us
  waiting for transfers between devices  129 us (43%)
  starting transfers between devices  59.5 us (20%)
  local copies, waits for them, and re-layouts  34.7 us (11%)
  matrix products  31.6 us (10%)
  other arithmetic  30.2 us (10%)
  Pallas kernels  15.6 us (5%)
    ppermute x34, waiting for transfers between devices, hop(): return lax.ppermute(v, 'dp', [(i, i ^ k) for i in range(n)])  65 us
    all_to_all x1, waiting for transfers between devices, body(): down_rows = lax.all_to_all(down_weight, 'dp', 0, 1, tiled=True)  42.5 us
    ppermute x34, starting transfers between devices, hop(): return lax.ppermute(v, 'dp', [(i, i ^ k) for i in range(n)])  36.2 us
    unnamed x74, local copies, waits for them, and re-layouts  22.4 us
    dot_general x11, matrix products, dot(): return jnp.dot(a, b, preferred_element_type=F32)  19.6 us
    ppermute x3, waiting for transfers between devices, up(): return lax.ppermute(v, 'dp', [(i, i + PLANE) for i in range(n - PLANE)])  14 us
    pallas_call x2, Pallas kernels, weigh(): pl.pallas_call(lambda *refs: weigh_kernel(count, *refs), grid=(size // ti...  13.6 us
    ppermute x3, starting transfers between devices, up(): return lax.ppermute(v, 'dp', [(i, i + PLANE) for i in range(n - PLANE)])  12.1 us
  transfers between devices with their start and end apart: 41, of which 21 were waited for; matrix products, arithmetic and copies ran while one was open for 21% of the time, Pallas kernels for 3%

profile of v2, /device:TPU:0, one launch (start us, length us, event | category | flops | bytes accessed | tf_op | source)
XLA Modules:
  0.0 302.4 jit_solution(10840823437400968242)
XLA Ops:
  0.7 7.4 %all-to-all-start = ((bf16[32,344,128]{2,1,0:T(8,128)(2,1)}), bf16[32,344,128]{2,1,0:T(8,128)(2,1)}, u32[]{:S(2)}, u32[]{:S(2)}) async-start(bf16[32,344,128]{2,1,0:T(8,128)(2,1)} %bitcast.77), calls=%async_computation | async-start | bytes 5636096 | tf_op jit(solution)/shard_map/all_to_all | solution.py:141
  8.4 10.9 %fusion = (bf16[4096,1024]{1,0:T(8,128)(2,1)}, bf16[4096,1024]{1,0:T(8,128)(2,1)}) fusion(bf16[4096,1024]{1,0:T(8,128)(2,1)} %param.11, f32[4096]{0:T(1024)S(1)} %copy-done.28), kind=kLoop, calls=%fused_computation.2 | loop fusion | flops 25165824 | bytes 25182208 | tf_op jit(solution)/shard_map/convert_element_type | solution.py:145
  21.3 2.4 fusion.20.position
  23.7 2.0 shard_map.86
  25.7 2.8 fusion.5
  30.0 42.5 %all-to-all-done = bf16[32,344,128]{2,1,0:T(8,128)(2,1)} async-done(((bf16[32,344,128]{2,1,0:T(8,128)(2,1)}), bf16[32,344,128]{2,1,0:T(8,128)(2,1)}, u32[]{:S(2)}, u32[]{:S(2)}) %all-to-all-start) | async-done | bytes 2818080 | tf_op jit(solution)/shard_map/all_to_all | solution.py:141
  72.5 2.3 copy_bitcast_fusion
  76.7 6.0 %fusion.43 = f32[344,1024]{1,0:T(8,128)S(1)} fusion(bf16[344,4096]{1,0:T(8,128)(2,1)S(1)} %copy_bitcast_fusion, bf16[4096,1024]{1,0:T(8,128)(2,1)} %get-tuple-element.21), kind=kOutput, calls=%fused_computation.119 | convolution fusion | flops 2885681152 | bytes 12615680 | tf_op jit(solution)/shard_map/dot_general | solution.py:18
  82.7 3.1 %add_convert_fusion = bf16[344,1024]{1,0:T(8,128)(2,1)S(1)} fusion(f32[344,1024]{1,0:T(8,128)S(1)} %fusion.43, bf16[344,4096]{1,0:T(8,128)(2,1)S(1)} %copy_bitcast_fusion, bf16[4096,1024]{1,0:T(8,128)(2,1)S(1)} %bitcast.75), kind=kOutput, calls=%fused_computation.21 | convolution fusion | flops 2886385664 | bytes 13320192 | tf_op jit(solution)/shard_map/dot_general | solution.py:18
  85.8 2.2 collective-permute-start.3
  89.3 2.2 collective-permute-start.7
  94.5 8.0 %collective-permute-done.3 = bf16[344,1024]{1,0:T(8,128)(2,1)} collective-permute-done((bf16[344,1024]{1,0:T(8,128)(2,1)S(1)}, bf16[344,1024]{1,0:T(8,128)(2,1)}, u32[]{:S(2)}, u32[]{:S(2)}) %collective-permute-start.3) | collective-permute-done | bytes 704544 | tf_op jit(solution)/shard_map/ppermute | solution.py:103
  102.5 5.3 %collective-permute-start.4 = (bf16[344,1024]{1,0:T(8,128)(2,1)}, bf16[344,1024]{1,0:T(8,128)(2,1)}, u32[]{:S(2)}, u32[]{:S(2)}) collective-permute-start(bf16[344,1024]{1,0:T(8,128)(2,1)} %collective-permute-done.3), channel_id=1, source_target_pairs={{0,8},{1,9},{2,10},{3,11},{4,12},{5,13},{6,14},{7,15},{8,16},{9,17... | collective-permute-start | bytes 2113544 | tf_op jit(solution)/shard_map/ppermute | solution.py:103
  109.2 8.0 %collective-permute-done.7 = bf16[4,2,176,344]{3,2,1,0:T(8,128)(2,1)S(1)} collective-permute-done((bf16[4,2,176,344]{3,2,1,0:T(8,128)(2,1)}, bf16[4,2,176,344]{3,2,1,0:T(8,128)(2,1)S(1)}, u32[]{:S(2)}, u32[]{:S(2)}) %collective-permute-start.7) | collective-permute-done | bytes 968736 | tf_op jit(solution)/shard_map/ppermute | solution.py:100
  117.2 4.7 %collective-permute-done.4 = bf16[344,1024]{1,0:T(8,128)(2,1)} collective-permute-done((bf16[344,1024]{1,0:T(8,128)(2,1)}, bf16[344,1024]{1,0:T(8,128)(2,1)}, u32[]{:S(2)}, u32[]{:S(2)}) %collective-permute-start.4) | collective-permute-done | bytes 704544 | tf_op jit(solution)/shard_map/ppermute | solution.py:103
  121.9 5.0 %collective-permute-done.6 = bf16[344,1024]{1,0:T(8,128)(2,1)} collective-permute-done((bf16[344,1024]{1,0:T(8,128)(2,1)}, bf16[344,1024]{1,0:T(8,128)(2,1)}, u32[]{:S(2)}, u32[]{:S(2)}) %collective-permute-start.6) | collective-permute-done | bytes 704544 | tf_op jit(solution)/shard_map/ppermute | solution.py:106
  128.2 4.6 %collective-permute-start.12 = (bf16[344,1024]{1,0:T(8,128)(2,1)}, bf16[344,1024]{1,0:T(8,128)(2,1)S(1)}, u32[]{:S(2)}, u32[]{:S(2)}) collective-permute-start(bf16[344,1024]{1,0:T(8,128)(2,1)} %collective-permute-done.4), channel_id=1, source_target_pairs={{0,8},{1,9},{2,10},{3,11},{4,12},{5,13},{6,14},{7,15},{8,16},{9,17... | collective-permute-start | bytes 2113544 | tf_op jit(solution)/shard_map/ppermute | solution.py:103
  132.8 6.1 %collective-permute-done.1 = bf16[4,2,176,344]{3,2,1,0:T(8,128)(2,1)} collective-permute-done((bf16[4,2,176,344]{3,2,1,0:T(8,128)(2,1)}, bf16[4,2,176,344]{3,2,1,0:T(8,128)(2,1)}, u32[]{:S(2)}, u32[]{:S(2)}) %collective-permute-start.1) | collective-permute-done | bytes 968736 | tf_op jit(solution)/shard_map/ppermute | solution.py:100
  139.4 2.0 pad_maximum_fusion
  142.3 3.0 collective-permute-done.11
  146.6 2.0 fusion.11
  156.4 1.9 collective-permute-start.14
  160.0 7.7 %collective-permute-done.14 = bf16[176,1024]{1,0:T(8,128)(2,1)S(1)} collective-permute-done((bf16[176,1024]{1,0:T(8,128)(2,1)S(1)}, bf16[176,1024]{1,0:T(8,128)(2,1)S(1)}, u32[]{:S(2)}, u32[]{:S(2)}) %collective-permute-start.14) | collective-permute-done | bytes 360480 | tf_op jit(solution)/shard_map/ppermute | solution.py:100
  167.7 8.9 %collective-permute-done.15 = bf16[176,1024]{1,0:T(8,128)(2,1)S(1)} collective-permute-done((bf16[176,1024]{1,0:T(8,128)(2,1)S(1)}, bf16[176,1024]{1,0:T(8,128)(2,1)S(1)}, u32[]{:S(2)}, u32[]{:S(2)}) %collective-permute-start.15) | collective-permute-done | bytes 360480 | tf_op jit(solution)/shard_map/ppermute | solution.py:100
  177.5 3.3 %collective-permute-start.24 = (bf16[176,1024]{1,0:T(8,128)(2,1)S(1)}, bf16[176,1024]{1,0:T(8,128)(2,1)S(1)}, u32[]{:S(2)}, u32[]{:S(2)}) collective-permute-start(bf16[176,1024]{1,0:T(8,128)(2,1)S(1)} %multiply_convert_fusion), channel_id=1, source_target_pairs={{0,16},{1,17},{2,18},{3,19},{4,20},{5,21},{6,22},{7,23},{8,24},{9,... | collective-permute-start | bytes 1081352 | tf_op jit(solution)/shard_map/ppermute | solution.py:100
  182.2 4.7 %collective-permute-done.17 = bf16[176,1024]{1,0:T(8,128)(2,1)S(1)} collective-permute-done((bf16[176,1024]{1,0:T(8,128)(2,1)S(1)}, bf16[176,1024]{1,0:T(8,128)(2,1)S(1)}, u32[]{:S(2)}, u32[]{:S(2)}) %collective-permute-start.17) | collective-permute-done | bytes 360480 | tf_op jit(solution)/shard_map/ppermute | solution.py:100
  187.4 8.5 %collective-permute-done.24 = bf16[176,1024]{1,0:T(8,128)(2,1)S(1)} collective-permute-done((bf16[176,1024]{1,0:T(8,128)(2,1)S(1)}, bf16[176,1024]{1,0:T(8,128)(2,1)S(1)}, u32[]{:S(2)}, u32[]{:S(2)}) %collective-permute-start.24) | collective-permute-done | bytes 360480 | tf_op jit(solution)/shard_map/ppermute | solution.py:100
  195.8 3.5 %collective-permute-start.28 = (bf16[176,1024]{1,0:T(8,128)(2,1)S(1)}, bf16[176,1024]{1,0:T(8,128)(2,1)}, u32[]{:S(2)}, u32[]{:S(2)}) collective-permute-start(bf16[176,1024]{1,0:T(8,128)(2,1)S(1)} %multiply_convert_fusion), channel_id=1, source_target_pairs={{0,24},{1,25},{2,26},{3,27},{4,28},{5,29},{6,30},{7,31},{8,16},{9,... | collective-permute-start | bytes 1081352 | tf_op jit(solution)/shard_map/ppermute | solution.py:100
  205.3 1.8 fusion.39
  212.6 1.8 constant_dynamic-update-slice_fusion.6
  214.4 4.1 %collective-permute-done.21 = bf16[176,1024]{1,0:T(8,128)(2,1)} collective-permute-done((bf16[176,1024]{1,0:T(8,128)(2,1)}, bf16[176,1024]{1,0:T(8,128)(2,1)}, u32[]{:S(2)}, u32[]{:S(2)}) %collective-permute-start.21) | collective-permute-done | bytes 360480 | tf_op jit(solution)/shard_map/ppermute | solution.py:100
  223.4 1.8 constant_dynamic-update-slice_fusion.5
  225.1 8.2 %collective-permute-done.27 = bf16[176,1024]{1,0:T(8,128)(2,1)S(1)} collective-permute-done((bf16[176,1024]{1,0:T(8,128)(2,1)}, bf16[176,1024]{1,0:T(8,128)(2,1)S(1)}, u32[]{:S(2)}, u32[]{:S(2)}) %collective-permute-start.27) | collective-permute-done | bytes 360480 | tf_op jit(solution)/shard_map/ppermute | solution.py:100
  234.1 6.2 %fusion.41 = (f32[704]{0:T(1024)}, f32[1024,704]{1,0:T(8,128)}) fusion(bf16[1024,1024]{1,0:T(8,128)(2,1)} %pad_maximum_fusion.1, bf16[704,1024]{1,0:T(8,128)(2,1)} %constant_dynamic-update-slice_fusion.4.refs_10_), kind=kOutput, calls=%fused_computation.117 | convolution fusion | flops 1477836032 | bytes 6425344 | tf_op jit(solution)/shard_map/dot_general | solution.py:181
  240.4 2.1 fusion.40
  246.7 2.4 exponential_reduce_fusion.1
  249.1 1.8 collective-permute-start.31
  255.6 2.7 collective-permute-done.31
  259.3 1.8 fusion.42
  261.2 1.7 copy-done.14
  263.5 1.8 collective-permute-start.32
  265.3 1.7 collective-permute-start.34
  267.3 1.7 collective-permute-done.33
  272.4 3.5 %collective-permute-start.37 = (f32[4,4,176]{2,1,0:T(4,128)S(1)}, f32[4,4,176]{2,1,0:T(4,128)S(1)}, u32[]{:S(2)}, u32[]{:S(2)}) collective-permute-start(f32[4,4,176]{2,1,0:T(4,128)S(1)} %log_add_fusion.1), channel_id=1, source_target_pairs={{0,24},{1,25},{2,26},{3,27},{4,28},{5,29},{6,30},{7,31},{8,16},{9,... | collective-permute-start | bytes 33800 | tf_op jit(solution)/shard_map/ppermute | solution.py:100
  275.9 2.0 collective-permute-done.37
  279.7 7.0 %shard_map.88 = (bf16[512,1024]{1,0:T(8,128)(2,1)}, f32[512,1]{1,0:T(8,128)S(1)}) custom-call(f32[1024,704]{1,0:T(8,128)} %copy-done.12, f32[1024,704]{1,0:T(8,128)} %copy-done.13, f32[1024,704]{1,0:T(8,128)} %get-tuple-element.82.refs_2_, f32[1024,704]{1,0:T(8,128)} %copy-done.14, f32[1,704]{1,0:T(1,128)S(1)} %reshape_squeeze.12.refs_4_, ...), custom_call_target="tpu_custom_call" | custom-call | flops 2952790016 | bytes 13631488 | tf_op jit(solution)/shard_map/pallas_call | solution.py:51
  291.5 6.6 %shard_map.87 = (f32[512,1024]{1,0:T(8,128)}, f32[512,1]{1,0:T(8,128)S(1)}) custom-call(f32[1024,704]{1,0:T(8,128)} %copy-done.12, f32[1024,704]{1,0:T(8,128)} %copy-done.13, f32[1024,704]{1,0:T(8,128)} %get-tuple-element.82.refs_2_, f32[1024,704]{1,0:T(8,128)} %copy-done.14, f32[1,704]{1,0:T(1,128)S(1)} %reshape_squeeze.12.refs_4_, ...), custom_call_target="tpu_custom_call" | custom-call | flops 2952790016 | bytes 13631488 | tf_op jit(solution)/shard_map/pallas_call | solution.py:51
  298.8 3.7 %add_multiply_fusion = f32[512,1024]{1,0:T(8,128)} fusion(f32[512,1024]{1,0:T(8,128)} %get-tuple-element.30, bf16[512,1024]{1,0:T(8,128)(2,1)} %collective-permute-done.38), kind=kLoop, calls=%fused_computation.15 | loop fusion | flops 1572864 | bytes 5242880 | tf_op jit(solution)/shard_map/mul | solution.py:200
  (175 shorter events, 65.7 us)
Async XLA Ops:
  0.6 25.1 %copy-start = (bf16[176,4096]{1,0:T(8,128)(2,1)S(1)}, bf16[176,4096]{1,0:T(8,128)(2,1)}, u32[]{:S(2)}) copy-start(bf16[176,4096]{1,0:T(8,128)(2,1)} %param.8) | copy-start | bytes 4325380
  0.7 71.8 %all-to-all-start = ((bf16[32,344,128]{2,1,0:T(8,128)(2,1)}), bf16[32,344,128]{2,1,0:T(8,128)(2,1)}, u32[]{:S(2)}, u32[]{:S(2)}) async-start(bf16[32,344,128]{2,1,0:T(8,128)(2,1)} %bitcast.77), calls=%async_computation | async-start | bytes 5636096 | tf_op jit(solution)/shard_map/all_to_all | solution.py:141
  8.1 20.4 %collective-permute-start = (bf16[512,1024]{1,0:T(8,128)(2,1)S(1)}, bf16[512,1024]{1,0:T(8,128)(2,1)S(1)}, u32[]{:S(2)}, u32[]{:S(2)}) collective-permute-start(bf16[512,1024]{1,0:T(8,128)(2,1)S(1)} %copy-done.21), channel_id=1, source_target_pairs={{0,1},{1,0},{2,3},{3,2},{4,5},{5,4},{6,7},{7,6},{8,9},{9,8},{10,11... | collective-permute-start | bytes 3145736 | tf_op jit(solution)/shard_map/ppermute | solution.py:100
  8.4 17.4 %copy-start.15 = (bf16[4096,1024]{1,0:T(8,128)(2,1)S(1)}, bf16[4096,1024]{1,0:T(8,128)(2,1)}, u32[]{:S(2)}) copy-start(bf16[4096,1024]{1,0:T(8,128)(2,1)} %param.11) | copy-start | bytes 25165828
  85.8 16.7 %collective-permute-start.3 = (bf16[344,1024]{1,0:T(8,128)(2,1)S(1)}, bf16[344,1024]{1,0:T(8,128)(2,1)}, u32[]{:S(2)}, u32[]{:S(2)}) collective-permute-start(bf16[344,1024]{1,0:T(8,128)(2,1)S(1)} %add_convert_fusion), channel_id=1, source_target_pairs={{0,8},{1,9},{2,10},{3,11},{4,12},{5,13},{6,14},{7,15},{8,16},{9,17... | collective-permute-start | bytes 2113544 | tf_op jit(solution)/shard_map/ppermute | solution.py:103
  88.0 19.9 %collective-permute-start.5 = (bf16[344,1024]{1,0:T(8,128)(2,1)S(1)}, bf16[344,1024]{1,0:T(8,128)(2,1)}, u32[]{:S(2)}, u32[]{:S(2)}) collective-permute-start(bf16[344,1024]{1,0:T(8,128)(2,1)S(1)} %add_convert_fusion), channel_id=1, source_target_pairs={{8,0},{9,1},{10,2},{11,3},{12,4},{13,5},{14,6},{15,7},{16,8},{17,9... | collective-permute-start | bytes 2113544 | tf_op jit(solution)/shard_map/ppermute | solution.py:106
  89.3 28.0 %collective-permute-start.7 = (bf16[4,2,176,344]{3,2,1,0:T(8,128)(2,1)}, bf16[4,2,176,344]{3,2,1,0:T(8,128)(2,1)S(1)}, u32[]{:S(2)}, u32[]{:S(2)}) collective-permute-start(bf16[4,2,176,344]{3,2,1,0:T(8,128)(2,1)} %slice_bitcast_fusion), channel_id=1, source_target_pairs={{0,6},{1,7},{2,4},{3,5},{4,2},{5,3},{6,0},{7,1},{8,14},{9,15},{10,... | collective-permute-start | bytes 2906120 | tf_op jit(solution)/shard_map/ppermute | solution.py:100
  93.2 45.7 %collective-permute-start.1 = (bf16[4,2,176,344]{3,2,1,0:T(8,128)(2,1)}, bf16[4,2,176,344]{3,2,1,0:T(8,128)(2,1)}, u32[]{:S(2)}, u32[]{:S(2)}) collective-permute-start(bf16[4,2,176,344]{3,2,1,0:T(8,128)(2,1)} %bitcast.10), channel_id=1, source_target_pairs={{0,2},{1,3},{2,0},{3,1},{4,6},{5,7},{6,4},{7,5},{8,10},{9,11},{10,... | collective-permute-start | bytes 2906120 | tf_op jit(solution)/shard_map/ppermute | solution.py:100
  93.7 45.7 %collective-permute-start.2 = (bf16[4,2,176,344]{3,2,1,0:T(8,128)(2,1)}, bf16[4,2,176,344]{3,2,1,0:T(8,128)(2,1)}, u32[]{:S(2)}, u32[]{:S(2)}) collective-permute-start(bf16[4,2,176,344]{3,2,1,0:T(8,128)(2,1)} %bitcast.11), channel_id=1, source_target_pairs={{0,4},{1,5},{2,6},{3,7},{4,0},{5,1},{6,2},{7,3},{8,12},{9,13},{10,... | collective-permute-start | bytes 2906120 | tf_op jit(solution)/shard_map/ppermute | solution.py:100
  102.5 19.4 %collective-permute-start.4 = (bf16[344,1024]{1,0:T(8,128)(2,1)}, bf16[344,1024]{1,0:T(8,128)(2,1)}, u32[]{:S(2)}, u32[]{:S(2)}) collective-permute-start(bf16[344,1024]{1,0:T(8,128)(2,1)} %collective-permute-done.3), channel_id=1, source_target_pairs={{0,8},{1,9},{2,10},{3,11},{4,12},{5,13},{6,14},{7,15},{8,16},{9,17... | collective-permute-start | bytes 2113544 | tf_op jit(solution)/shard_map/ppermute | solution.py:103
  107.9 19.0 %collective-permute-start.6 = (bf16[344,1024]{1,0:T(8,128)(2,1)}, bf16[344,1024]{1,0:T(8,128)(2,1)}, u32[]{:S(2)}, u32[]{:S(2)}) collective-permute-start(bf16[344,1024]{1,0:T(8,128)(2,1)} %collective-permute-done.5), channel_id=1, source_target_pairs={{8,0},{9,1},{10,2},{11,3},{12,4},{13,5},{14,6},{15,7},{16,8},{17,9... | collective-permute-start | bytes 2113544 | tf_op jit(solution)/shard_map/ppermute | solution.py:106
  117.2 31.5 %collective-permute-start.8 = (bf16[344,1024]{1,0:T(8,128)(2,1)S(1)}, bf16[344,1024]{1,0:T(8,128)(2,1)S(1)}, u32[]{:S(2)}, u32[]{:S(2)}) collective-permute-start(bf16[344,1024]{1,0:T(8,128)(2,1)S(1)} %add_convert_fusion), channel_id=1, source_target_pairs={{0,1},{1,0},{2,3},{3,2},{4,5},{5,4},{6,7},{7,6},{8,9},{9,8},{10,11... | collective-permute-start | bytes 2113544 | tf_op jit(solution)/shard_map/ppermute | solution.py:100
  126.9 18.4 %collective-permute-start.11 = (bf16[344,1024]{1,0:T(8,128)(2,1)}, bf16[344,1024]{1,0:T(8,128)(2,1)S(1)}, u32[]{:S(2)}, u32[]{:S(2)}) collective-permute-start(bf16[344,1024]{1,0:T(8,128)(2,1)} %collective-permute-done.6), channel_id=1, source_target_pairs={{8,0},{9,1},{10,2},{11,3},{12,4},{13,5},{14,6},{15,7},{16,8},{17,9... | collective-permute-start | bytes 2113544 | tf_op jit(solution)/shard_map/ppermute | solution.py:106
  128.2 18.4 %collective-permute-start.12 = (bf16[344,1024]{1,0:T(8,128)(2,1)}, bf16[344,1024]{1,0:T(8,128)(2,1)S(1)}, u32[]{:S(2)}, u32[]{:S(2)}) collective-permute-start(bf16[344,1024]{1,0:T(8,128)(2,1)} %collective-permute-done.4), channel_id=1, source_target_pairs={{0,8},{1,9},{2,10},{3,11},{4,12},{5,13},{6,14},{7,15},{8,16},{9,17... | collective-permute-start | bytes 2113544 | tf_op jit(solution)/shard_map/ppermute | solution.py:103
  148.6 3.5 %collective-permute-start.9 = (bf16[344,1024]{1,0:T(8,128)(2,1)S(1)}, bf16[344,1024]{1,0:T(8,128)(2,1)S(1)}, u32[]{:S(2)}, u32[]{:S(2)}) collective-permute-start(bf16[344,1024]{1,0:T(8,128)(2,1)S(1)} %get-tuple-element.46), channel_id=1, source_target_pairs={{0,1},{1,0},{2,3},{3,2},{4,5},{5,4},{6,7},{7,6},{8,9},{9,8},{10,11... | collective-permute-start | bytes 2113544 | tf_op jit(solution)/shard_map/ppermute | solution.py:100
  149.6 3.4 %collective-permute-start.10 = (bf16[344,1024]{1,0:T(8,128)(2,1)S(1)}, bf16[344,1024]{1,0:T(8,128)(2,1)S(1)}, u32[]{:S(2)}, u32[]{:S(2)}) collective-permute-start(bf16[344,1024]{1,0:T(8,128)(2,1)S(1)} %get-tuple-element.44), channel_id=1, source_target_pairs={{0,1},{1,0},{2,3},{3,2},{4,5},{5,4},{6,7},{7,6},{8,9},{9,8},{10,11... | collective-permute-start | bytes 2113544 | tf_op jit(solution)/shard_map/ppermute | solution.py:100
  151.1 2.9 collective-permute-start.13
  154.9 21.8 %copy-start.22 = (f32[176,1024]{1,0:T(8,128)S(1)}, f32[176,1024]{1,0:T(8,128)}, u32[]{:S(2)}) copy-start(f32[176,1024]{1,0:T(8,128)} %fusion.5) | copy-start | bytes 2162692
  156.4 11.3 %collective-permute-start.14 = (bf16[176,1024]{1,0:T(8,128)(2,1)S(1)}, bf16[176,1024]{1,0:T(8,128)(2,1)S(1)}, u32[]{:S(2)}, u32[]{:S(2)}) collective-permute-start(bf16[176,1024]{1,0:T(8,128)(2,1)S(1)} %get-tuple-element.41), channel_id=1, source_target_pairs={{0,2},{1,3},{2,0},{3,1},{4,6},{5,7},{6,4},{7,5},{8,10},{9,11},{10,... | collective-permute-start | bytes 1081352 | tf_op jit(solution)/shard_map/ppermute | solution.py:100
  158.4 18.2 %collective-permute-start.15 = (bf16[176,1024]{1,0:T(8,128)(2,1)S(1)}, bf16[176,1024]{1,0:T(8,128)(2,1)S(1)}, u32[]{:S(2)}, u32[]{:S(2)}) collective-permute-start(bf16[176,1024]{1,0:T(8,128)(2,1)S(1)} %get-tuple-element.43), channel_id=1, source_target_pairs={{0,4},{1,5},{2,6},{3,7},{4,0},{5,1},{6,2},{7,3},{8,12},{9,13},{10,... | collective-permute-start | bytes 1081352 | tf_op jit(solution)/shard_map/ppermute | solution.py:100
  158.4 18.2 %collective-permute-start.16 = (bf16[176,1024]{1,0:T(8,128)(2,1)S(1)}, bf16[176,1024]{1,0:T(8,128)(2,1)S(1)}, u32[]{:S(2)}, u32[]{:S(2)}) collective-permute-start(bf16[176,1024]{1,0:T(8,128)(2,1)S(1)} %get-tuple-element.42), channel_id=1, source_target_pairs={{0,6},{1,7},{2,4},{3,5},{4,2},{5,3},{6,0},{7,1},{8,14},{9,15},{10,... | collective-permute-start | bytes 1081352 | tf_op jit(solution)/shard_map/ppermute | solution.py:100
  176.6 28.6 %copy-start.16 = (bf16[1024,1024]{1,0:T(8,128)(2,1)S(1)}, bf16[1024,1024]{1,0:T(8,128)(2,1)}, u32[]{:S(2)}) copy-start(bf16[1024,1024]{1,0:T(8,128)(2,1)} %pad_maximum_fusion.1) | copy-start | bytes 6291460
  177.1 30.0 %copy-start.19 = (bf16[176,1024]{1,0:T(8,128)(2,1)}, bf16[176,1024]{1,0:T(8,128)(2,1)S(1)}, u32[]{:S(2)}) copy-start(bf16[176,1024]{1,0:T(8,128)(2,1)S(1)} %multiply_convert_fusion) | copy-start | bytes 1081348
  177.1 9.8 %collective-permute-start.17 = (bf16[176,1024]{1,0:T(8,128)(2,1)S(1)}, bf16[176,1024]{1,0:T(8,128)(2,1)S(1)}, u32[]{:S(2)}, u32[]{:S(2)}) collective-permute-start(bf16[176,1024]{1,0:T(8,128)(2,1)S(1)} %multiply_convert_fusion), channel_id=1, source_target_pairs={{0,2},{1,3},{2,0},{3,1},{4,6},{5,7},{6,4},{7,5},{8,10},{9,11},{10,... | collective-permute-start | bytes 1081352 | tf_op jit(solution)/shard_map/ppermute | solution.py:100
  177.5 18.3 %collective-permute-start.24 = (bf16[176,1024]{1,0:T(8,128)(2,1)S(1)}, bf16[176,1024]{1,0:T(8,128)(2,1)S(1)}, u32[]{:S(2)}, u32[]{:S(2)}) collective-permute-start(bf16[176,1024]{1,0:T(8,128)(2,1)S(1)} %multiply_convert_fusion), channel_id=1, source_target_pairs={{0,16},{1,17},{2,18},{3,19},{4,20},{5,21},{6,22},{7,23},{8,24},{9,... | collective-permute-start | bytes 1081352 | tf_op jit(solution)/shard_map/ppermute | solution.py:100
  180.9 19.9 %collective-permute-start.20 = (bf16[176,1024]{1,0:T(8,128)(2,1)S(1)}, bf16[176,1024]{1,0:T(8,128)(2,1)}, u32[]{:S(2)}, u32[]{:S(2)}) collective-permute-start(bf16[176,1024]{1,0:T(8,128)(2,1)S(1)} %multiply_convert_fusion), channel_id=1, source_target_pairs={{0,8},{1,9},{2,10},{3,11},{4,12},{5,13},{6,14},{7,15},{8,0},{9,1},... | collective-permute-start | bytes 1081352 | tf_op jit(solution)/shard_map/ppermute | solution.py:100
  181.6 21.7 %collective-permute-start.18 = (bf16[176,1024]{1,0:T(8,128)(2,1)S(1)}, bf16[176,1024]{1,0:T(8,128)(2,1)S(1)}, u32[]{:S(2)}, u32[]{:S(2)}) collective-permute-start(bf16[176,1024]{1,0:T(8,128)(2,1)S(1)} %multiply_convert_fusion), channel_id=1, source_target_pairs={{0,4},{1,5},{2,6},{3,7},{4,0},{5,1},{6,2},{7,3},{8,12},{9,13},{10,... | collective-permute-start | bytes 1081352 | tf_op jit(solution)/shard_map/ppermute | solution.py:100
  186.9 20.3 %copy-start.23 = (bf16[176,1024]{1,0:T(8,128)(2,1)}, bf16[176,1024]{1,0:T(8,128)(2,1)S(1)}, u32[]{:S(2)}) copy-start(bf16[176,1024]{1,0:T(8,128)(2,1)S(1)} %collective-permute-done.17) | copy-start | bytes 1081348
  186.9 17.1 %collective-permute-start.19 = (bf16[176,1024]{1,0:T(8,128)(2,1)S(1)}, bf16[176,1024]{1,0:T(8,128)(2,1)S(1)}, u32[]{:S(2)}, u32[]{:S(2)}) collective-permute-start(bf16[176,1024]{1,0:T(8,128)(2,1)S(1)} %collective-permute-done.17), channel_id=1, source_target_pairs={{0,4},{1,5},{2,6},{3,7},{4,0},{5,1},{6,2},{7,3},{8,12},{9,13},{10,... | collective-permute-start | bytes 1081352 | tf_op jit(solution)/shard_map/ppermute | solution.py:100
  195.8 13.5 %collective-permute-start.28 = (bf16[176,1024]{1,0:T(8,128)(2,1)S(1)}, bf16[176,1024]{1,0:T(8,128)(2,1)}, u32[]{:S(2)}, u32[]{:S(2)}) collective-permute-start(bf16[176,1024]{1,0:T(8,128)(2,1)S(1)} %multiply_convert_fusion), channel_id=1, source_target_pairs={{0,24},{1,25},{2,26},{3,27},{4,28},{5,29},{6,30},{7,31},{8,16},{9,... | collective-permute-start | bytes 1081352 | tf_op jit(solution)/shard_map/ppermute | solution.py:100
  199.4 11.7 %collective-permute-start.25 = (bf16[176,1024]{1,0:T(8,128)(2,1)S(1)}, bf16[176,1024]{1,0:T(8,128)(2,1)}, u32[]{:S(2)}, u32[]{:S(2)}) collective-permute-start(bf16[176,1024]{1,0:T(8,128)(2,1)S(1)} %collective-permute-done.24), channel_id=1, source_target_pairs={{0,2},{1,3},{2,0},{3,1},{4,6},{5,7},{6,4},{7,5},{8,10},{9,11},{10,... | collective-permute-start | bytes 1081352 | tf_op jit(solution)/shard_map/ppermute | solution.py:100
  200.7 22.6 %collective-permute-start.26 = (bf16[176,1024]{1,0:T(8,128)(2,1)S(1)}, bf16[176,1024]{1,0:T(8,128)(2,1)}, u32[]{:S(2)}, u32[]{:S(2)}) collective-permute-start(bf16[176,1024]{1,0:T(8,128)(2,1)S(1)} %collective-permute-done.24), channel_id=1, source_target_pairs={{0,4},{1,5},{2,6},{3,7},{4,0},{5,1},{6,2},{7,3},{8,12},{9,13},{10,... | collective-permute-start | bytes 1081352 | tf_op jit(solution)/shard_map/ppermute | solution.py:100
  203.2 15.3 %collective-permute-start.21 = (bf16[176,1024]{1,0:T(8,128)(2,1)}, bf16[176,1024]{1,0:T(8,128)(2,1)}, u32[]{:S(2)}, u32[]{:S(2)}) collective-permute-start(bf16[176,1024]{1,0:T(8,128)(2,1)} %collective-permute-done.20), channel_id=1, source_target_pairs={{0,2},{1,3},{2,0},{3,1},{4,6},{5,7},{6,4},{7,5},{8,10},{9,11},{10,... | collective-permute-start | bytes 1081352 | tf_op jit(solution)/shard_map/ppermute | solution.py:100
  204.0 15.9 %collective-permute-start.22 = (bf16[176,1024]{1,0:T(8,128)(2,1)}, bf16[176,1024]{1,0:T(8,128)(2,1)}, u32[]{:S(2)}, u32[]{:S(2)}) collective-permute-start(bf16[176,1024]{1,0:T(8,128)(2,1)} %collective-permute-done.20), channel_id=1, source_target_pairs={{0,4},{1,5},{2,6},{3,7},{4,0},{5,1},{6,2},{7,3},{8,12},{9,13},{10,... | collective-permute-start | bytes 1081352 | tf_op jit(solution)/shard_map/ppermute | solution.py:100
  209.4 44.2 %collective-permute-start.29 = (bf16[176,1024]{1,0:T(8,128)(2,1)}, bf16[176,1024]{1,0:T(8,128)(2,1)}, u32[]{:S(2)}, u32[]{:S(2)}) collective-permute-start(bf16[176,1024]{1,0:T(8,128)(2,1)} %collective-permute-done.28), channel_id=1, source_target_pairs={{0,2},{1,3},{2,0},{3,1},{4,6},{5,7},{6,4},{7,5},{8,10},{9,11},{10,... | collective-permute-start | bytes 1081352 | tf_op jit(solution)/shard_map/ppermute | solution.py:100
  211.1 38.0 %collective-permute-start.30 = (bf16[176,1024]{1,0:T(8,128)(2,1)}, bf16[176,1024]{1,0:T(8,128)(2,1)}, u32[]{:S(2)}, u32[]{:S(2)}) collective-permute-start(bf16[176,1024]{1,0:T(8,128)(2,1)} %collective-permute-done.28), channel_id=1, source_target_pairs={{0,4},{1,5},{2,6},{3,7},{4,0},{5,1},{6,2},{7,3},{8,12},{9,13},{10,... | collective-permute-start | bytes 1081352 | tf_op jit(solution)/shard_map/ppermute | solution.py:100
  218.5 14.8 %collective-permute-start.27 = (bf16[176,1024]{1,0:T(8,128)(2,1)}, bf16[176,1024]{1,0:T(8,128)(2,1)S(1)}, u32[]{:S(2)}, u32[]{:S(2)}) collective-permute-start(bf16[176,1024]{1,0:T(8,128)(2,1)} %collective-permute-done.25), channel_id=1, source_target_pairs={{0,4},{1,5},{2,6},{3,7},{4,0},{5,1},{6,2},{7,3},{8,12},{9,13},{10,... | collective-permute-start | bytes 1081352 | tf_op jit(solution)/shard_map/ppermute | solution.py:100
  219.9 20.4 %collective-permute-start.23 = (bf16[176,1024]{1,0:T(8,128)(2,1)}, bf16[176,1024]{1,0:T(8,128)(2,1)S(1)}, u32[]{:S(2)}, u32[]{:S(2)}) collective-permute-start(bf16[176,1024]{1,0:T(8,128)(2,1)} %collective-permute-done.22), channel_id=1, source_target_pairs={{0,2},{1,3},{2,0},{3,1},{4,6},{5,7},{6,4},{7,5},{8,10},{9,11},{10,... | collective-permute-start | bytes 1081352 | tf_op jit(solution)/shard_map/ppermute | solution.py:100
  249.1 9.2 %collective-permute-start.31 = (bf16[176,1024]{1,0:T(8,128)(2,1)}, bf16[176,1024]{1,0:T(8,128)(2,1)}, u32[]{:S(2)}, u32[]{:S(2)}) collective-permute-start(bf16[176,1024]{1,0:T(8,128)(2,1)} %collective-permute-done.30), channel_id=1, source_target_pairs={{0,2},{1,3},{2,0},{3,1},{4,6},{5,7},{6,4},{7,5},{8,10},{9,11},{10,... | collective-permute-start | bytes 1081352 | tf_op jit(solution)/shard_map/ppermute | solution.py:100
  262.9 15.4 %copy-start.7 = (bf16[704,1024]{1,0:T(8,128)(2,1)S(1)}, bf16[704,1024]{1,0:T(8,128)(2,1)}, u32[]{:S(2)}) copy-start(bf16[704,1024]{1,0:T(8,128)(2,1)} %copy-done.6) | copy-start | bytes 4325380
  263.5 3.8 %collective-permute-start.32 = (f32[4,4,176]{2,1,0:T(4,128)S(1)}, f32[4,4,176]{2,1,0:T(4,128)S(1)}, u32[]{:S(2)}, u32[]{:S(2)}) collective-permute-start(f32[4,4,176]{2,1,0:T(4,128)S(1)} %constant_dynamic-update-slice_fusion.12), channel_id=1, source_target_pairs={{0,2},{1,3},{2,0},{3,1},{4,6},{5,7},{6,4},{7,5},{8,10},{9,11},{10,... | collective-permute-start | bytes 33800 | tf_op jit(solution)/shard_map/ppermute | solution.py:100
  265.3 3.7 %collective-permute-start.33 = (f32[4,4,176]{2,1,0:T(4,128)S(1)}, f32[4,4,176]{2,1,0:T(4,128)S(1)}, u32[]{:S(2)}, u32[]{:S(2)}) collective-permute-start(f32[4,4,176]{2,1,0:T(4,128)S(1)} %constant_dynamic-update-slice_fusion.12), channel_id=1, source_target_pairs={{0,4},{1,5},{2,6},{3,7},{4,0},{5,1},{6,2},{7,3},{8,12},{9,13},{10,... | collective-permute-start | bytes 33800 | tf_op jit(solution)/shard_map/ppermute | solution.py:100
  265.3 4.6 %collective-permute-start.34 = (f32[4,4,176]{2,1,0:T(4,128)S(1)}, f32[4,4,176]{2,1,0:T(4,128)S(1)}, u32[]{:S(2)}, u32[]{:S(2)}) collective-permute-start(f32[4,4,176]{2,1,0:T(4,128)S(1)} %constant_dynamic-update-slice_fusion.12), channel_id=1, source_target_pairs={{0,6},{1,7},{2,4},{3,5},{4,2},{5,3},{6,0},{7,1},{8,14},{9,15},{10,... | collective-permute-start | bytes 33800 | tf_op jit(solution)/shard_map/ppermute | solution.py:100
  270.1 5.8 %collective-permute-start.36 = (f32[4,4,176]{2,1,0:T(4,128)S(1)}, f32[4,4,176]{2,1,0:T(4,128)S(1)}, u32[]{:S(2)}, u32[]{:S(2)}) collective-permute-start(f32[4,4,176]{2,1,0:T(4,128)S(1)} %log_add_fusion.1), channel_id=1, source_target_pairs={{0,16},{1,17},{2,18},{3,19},{4,20},{5,21},{6,22},{7,23},{8,24},{9,... | collective-permute-start | bytes 33800 | tf_op jit(solution)/shard_map/ppermute | solution.py:100
  271.5 4.4 %collective-permute-start.35 = (f32[4,4,176]{2,1,0:T(4,128)S(1)}, f32[4,4,176]{2,1,0:T(4,128)S(1)}, u32[]{:S(2)}, u32[]{:S(2)}) collective-permute-start(f32[4,4,176]{2,1,0:T(4,128)S(1)} %log_add_fusion.1), channel_id=1, source_target_pairs={{0,8},{1,9},{2,10},{3,11},{4,12},{5,13},{6,14},{7,15},{8,0},{9,1},... | collective-permute-start | bytes 33800 | tf_op jit(solution)/shard_map/ppermute | solution.py:100
  272.4 5.5 %collective-permute-start.37 = (f32[4,4,176]{2,1,0:T(4,128)S(1)}, f32[4,4,176]{2,1,0:T(4,128)S(1)}, u32[]{:S(2)}, u32[]{:S(2)}) collective-permute-start(f32[4,4,176]{2,1,0:T(4,128)S(1)} %log_add_fusion.1), channel_id=1, source_target_pairs={{0,24},{1,25},{2,26},{3,27},{4,28},{5,29},{6,30},{7,31},{8,16},{9,... | collective-permute-start | bytes 33800 | tf_op jit(solution)/shard_map/ppermute | solution.py:100
  286.7 12.1 %collective-permute-start.38 = (bf16[512,1024]{1,0:T(8,128)(2,1)}, bf16[512,1024]{1,0:T(8,128)(2,1)}, u32[]{:S(2)}, u32[]{:S(2)}) collective-permute-start(bf16[512,1024]{1,0:T(8,128)(2,1)} %get-tuple-element.31), channel_id=1, source_target_pairs={{0,1},{1,0},{2,3},{3,2},{4,5},{5,4},{6,7},{7,6},{8,9},{9,8},{10,11... | collective-permute-start | bytes 3145736 | tf_op jit(solution)/shard_map/ppermute | solution.py:100
  286.8 11.4 %collective-permute-start.39 = (f32[512]{0:T(512)S(1)}, f32[512]{0:T(512)S(1)}, u32[]{:S(2)}, u32[]{:S(2)}) collective-permute-start(f32[512]{0:T(512)S(1)} %reduce.1), channel_id=1, source_target_pairs={{0,1},{1,0},{2,3},{3,2},{4,5},{5,4},{6,7},{7,6},{8,9},{9,8},{10,11... | collective-permute-start | bytes 6152 | tf_op jit(solution)/shard_map/ppermute | solution.py:100
  (24 other events, 120.8 us)
